TPU v7x, 128 devices: a whole 4x4x4 slice. The times are simulated.
128 devices in a mesh: fsdp: 16 (over y_lo, z, core), tp: 8 (over x, y_hi).
Axes of the slice: x: 4, y: 4 (y_hi: 2, y_lo: 2; y = y_hi * 2 + y_lo), z: 4, core: 2. Of those that a mesh axis runs over, the one named last changes fastest.
Arguments:
- hidden_in: bfloat16 [1024, 4096], P('fsdp'), may hold values from -3 to 3
- queries: bfloat16 [2, 1024, 8192], P(None, ('fsdp', 'tp')), may hold values from -170 to 170
- key_cache: bfloat16 [1024, 256, 512], P(('fsdp', 'tp')), may hold values from -6 to 6
- value_cache: bfloat16 [1024, 256, 512], P(('fsdp', 'tp')), may hold values from -6 to 6
- new_keys: bfloat16 [2, 1024, 512], P(None, ('fsdp', 'tp')), may hold values from -6 to 6
- new_values: bfloat16 [2, 1024, 512], P(None, ('fsdp', 'tp')), may hold values from -6 to 6
- lengths: int32 [1024], P(('fsdp', 'tp')), may hold values from 2 to 256
- routes: int32 [2, 1024, 8], P(None, 'fsdp'), may hold values from 0 to 127, all different within a row; in each aligned block of 64 rows (0 to 63, 64 to 127, ..., all dimensions but the last counted through in order) at most 8 rows name the same one
- route_weights: float32 [2, 1024, 8], P(None, 'fsdp'), may hold values from 0.05 to 1
- norm_gain: float32 [4096], replicated, may hold values from 0.1 to 1.9
- gate_master: float32 [8, 1536, 4096], P(None, ('fsdp', 'tp')), may hold values from -0.09375 to 0.09375
- up_master: float32 [8, 1536, 4096], P(None, ('fsdp', 'tp')), may hold values from -0.09375 to 0.09375
- down_master: float32 [8, 1536, 4096], P(None, ('fsdp', 'tp')), may hold values from -0.3125 to 0.3125
- out_proj: bfloat16 [8192, 4096], P('tp'), may hold values from -0.0625 to 0.0625
Outputs:
- hidden_out: bfloat16 [1024, 4096], P('fsdp', 'tp')
- scale_log2: float32 [3, 8, 12, 32], replicated
Inputs may be any that keep to these rules, and one draw needn't show every extreme that they name: `routes`: within one step and one index of fsdp (aligned blocks of 64 rows), no expert is named by more than 8 rows.
All inputs are finite; a program needn't handle non-finite values.
Results may differ from a plain program's by a relative error of at most 0.0095.
Values may be sent and summed in bfloat16 or wider, within the bound.
A program may use at most 256 MiB of HBM per device.

v0:
```python
import jax
import jax.numpy as jnp
from jax import lax
from jax.sharding import PartitionSpec as P

D = 4096
FF = 1536
QH = 64
KVH = 4
HD = 128
BLOCK = 128
WIN = 8
CAP = 8


neg_fill = -1e30
epsilon = 1e-06
fp_limit = 448.0
grid_floor = 2.0 ** (-10)
least_exponent = -6.0


def cut_along(array, dim, peers):
    before, after = (array.shape[:dim], array.shape[dim + 1 :])
    return jnp.moveaxis(array.reshape(*before, peers, -1, *after), dim, 0)


def sent_and_summed(array, axis, dim):
    blocks = cut_along(array, dim, lax.axis_size(axis))
    arrived = lax.all_to_all(blocks, axis, split_axis=0, concat_axis=0, tiled=True)
    return arrived.astype(jnp.float32).sum(axis=0)


def copy_for_each(array, axis):
    peers = lax.axis_size(axis)
    return lax.all_to_all(
        jnp.broadcast_to(array[None], (peers, *array.shape)), axis, 0, 0, tiled=True
    )


def joined_along(blocks, dim):
    blocks = jnp.moveaxis(blocks, 0, dim)
    lengths = blocks.shape
    return blocks.reshape(*lengths[:dim], lengths[dim] * lengths[dim + 1], *lengths[dim + 2 :])


def collect(array, axis, dim):
    blocks = copy_for_each(array, axis)
    return joined_along(blocks, dim)


def grid_round(values):
    magnitude = jnp.abs(values)
    exponent = jnp.maximum(jnp.floor(jnp.log2(jnp.maximum(magnitude, grid_floor))), least_exponent)
    spacing = jnp.exp2(exponent - 3.0)
    return jnp.sign(values) * jnp.floor(magnitude / spacing + 0.5) * spacing


def row_scales(scales, owner_map):
    return jnp.einsum(
        "sb,xwbc->xwsc", owner_map.astype(jnp.float32), scales, precision=lax.Precision.HIGHEST
    )


def owner_blocks(owner_rows):
    return (owner_rows // BLOCK)[:, None] == jnp.arange(FF // BLOCK, dtype=jnp.int32)[None, :]


def dequantize(shard_piece, shard_rows, tp_count, tp_pos, scales):
    count = shard_piece.shape[2]
    gathered_index = jnp.arange(count, dtype=jnp.int32)
    owner_rows = (
        gathered_index // shard_rows * tp_count + tp_pos
    ) * shard_rows + gathered_index % shard_rows
    factors = row_scales(scales, owner_blocks(owner_rows))
    tiles = shard_piece.astype(jnp.float32).reshape(3, WIN, count, D // BLOCK, BLOCK)
    return (tiles * factors[..., None]).astype(jnp.bfloat16).reshape(3, WIN, count, D)


def attention_rows(queries_now, cache_keys, cache_values, fresh_keys, fresh_values, lengths):
    row_count = queries_now.shape[0]
    positions = cache_keys.shape[1]
    group = QH // KVH
    score_scale = HD ** (-0.5)
    fresh_count = fresh_keys.shape[0]
    query_heads = queries_now.reshape(row_count, KVH, group, HD)
    key_heads = cache_keys.reshape(row_count, positions, KVH, HD)
    value_heads = cache_values.reshape(row_count, positions, KVH, HD)
    fresh_key_heads = fresh_keys.reshape(fresh_count, row_count, KVH, HD)
    fresh_value_heads = fresh_values.reshape(fresh_count, row_count, KVH, HD)
    cached_scores = (
        jnp.einsum("rkgd,rpkd->rkgp", query_heads, key_heads, preferred_element_type=jnp.float32)
        * score_scale
    )
    fresh_scores = (
        jnp.einsum(
            "rkgd,srkd->rkgs", query_heads, fresh_key_heads, preferred_element_type=jnp.float32
        )
        * score_scale
    )
    alive_mask = (jnp.arange(positions, dtype=jnp.int32)[None, :] < lengths[:, None])[
        :, None, None, :
    ]
    peak_score = jnp.maximum(
        jnp.max(jnp.where(alive_mask, cached_scores, neg_fill), axis=-1),
        jnp.max(fresh_scores, axis=-1),
    )
    cached_weights = jnp.where(alive_mask, jnp.exp(cached_scores - peak_score[..., None]), 0.0)
    fresh_weights = jnp.exp(fresh_scores - peak_score[..., None])
    weight_sum = jnp.sum(cached_weights, axis=-1) + jnp.sum(fresh_weights, axis=-1)
    cached_probs = (cached_weights / weight_sum[..., None]).astype(jnp.bfloat16)
    fresh_probs = (fresh_weights / weight_sum[..., None]).astype(jnp.bfloat16)
    output = jnp.einsum(
        "rkgp,rpkd->rkgd", cached_probs, value_heads, preferred_element_type=jnp.float32
    )
    output = output + jnp.einsum(
        "rkgs,srkd->rkgd", fresh_probs, fresh_value_heads, preferred_element_type=jnp.float32
    )
    return output.astype(jnp.bfloat16).reshape(row_count, QH * HD)


def routing_tables(routes, route_weights, capacity):
    weight_sum = jnp.sum(route_weights, axis=1)
    experts = jnp.arange(WIN, dtype=jnp.int32)
    matches = routes[None, :, :] == experts[:, None, None]
    chosen = jnp.any(matches, axis=2)
    gate_share = (
        jnp.sum(jnp.where(matches, route_weights[None, :, :], 0.0), axis=2) / weight_sum[None, :]
    )
    slot_index = jnp.cumsum(chosen.astype(jnp.int32), axis=1) - 1
    places = jnp.arange(capacity, dtype=jnp.int32)
    picked = (slot_index[:, None, :] == places[None, :, None]) & chosen[:, None, :]
    return (picked.astype(jnp.bfloat16), picked.astype(jnp.float32) * gate_share[:, None, :])


def expert_rows(selected, gate_rows, up_rows, down_rows):
    gate_act = jnp.einsum("ecd,ehd->ech", selected, gate_rows, preferred_element_type=jnp.float32)
    up_act = jnp.einsum("ecd,ehd->ech", selected, up_rows, preferred_element_type=jnp.float32)
    product = (jax.nn.silu(gate_act) * up_act).astype(jnp.bfloat16)
    return jnp.einsum("ech,ehd->ecd", product, down_rows, preferred_element_type=jnp.float32)


def local_experts(selected, weighted, restored):
    outputs = expert_rows(selected, restored[0], restored[1], restored[2])
    return jnp.einsum("ecr,ecd->rd", weighted, outputs, precision=lax.Precision.HIGHEST)


def local(
    hidden_in,
    queries,
    key_cache,
    value_cache,
    new_keys,
    new_values,
    lengths,
    routes,
    route_weights,
    norm_gain,
    gate_master,
    up_master,
    down_master,
    out_proj,
):
    tp_count = lax.axis_size("tp")
    fsdp_pos = lax.axis_index("fsdp")
    tp_pos = lax.axis_index("tp")
    shard_rows = gate_master.shape[1]
    masters = jnp.stack([gate_master, up_master, down_master])
    owned_rows = (fsdp_pos * tp_count + tp_pos) * shard_rows + jnp.arange(
        shard_rows, dtype=jnp.int32
    )
    owner_map = owner_blocks(owned_rows)
    magnitude = jnp.max(jnp.abs(masters).reshape(3, WIN, shard_rows, D // BLOCK, BLOCK), axis=4)
    partial_max = jnp.max(
        jnp.where(owner_map[None, None, :, :, None], magnitude[:, :, :, None, :], 0.0), axis=2
    )
    block_max = lax.pmax(partial_max, ("fsdp", "tp"))
    scales = (block_max + epsilon) / fp_limit
    scale_log2 = jnp.log2(scales)
    local_factors = row_scales(scales, owner_map)
    tiles = masters.reshape(3, WIN, shard_rows, D // BLOCK, BLOCK)
    quantized = (
        grid_round(tiles / local_factors[..., None])
        .astype(jnp.bfloat16)
        .reshape(3, WIN, shard_rows, D)
    )
    gathered = lax.all_gather(quantized, "fsdp", axis=2, tiled=True)
    restored = dequantize(gathered, shard_rows, tp_count, tp_pos, scales)
    share_cols = D // tp_count
    own_start = tp_pos * share_cols
    current = lax.dynamic_slice_in_dim(hidden_in, own_start, share_cols, 1)
    for step_index in range(2):
        heads_local = attention_rows(
            queries[step_index],
            key_cache,
            value_cache,
            new_keys[: step_index + 1],
            new_values[: step_index + 1],
            lengths,
        )
        regrouped = lax.all_to_all(heads_local, "tp", split_axis=1, concat_axis=0, tiled=True)
        projected = jnp.dot(regrouped, out_proj, preferred_element_type=jnp.float32)
        mixed = (
            current.astype(jnp.float32) + sent_and_summed(projected.astype(jnp.bfloat16), "tp", 1)
        ).astype(jnp.bfloat16)
        values = mixed.astype(jnp.float32)
        squares = lax.psum(jnp.sum(values * values, axis=1), "tp")
        inverse = lax.rsqrt(squares / D + epsilon)
        own_gain = lax.dynamic_slice_in_dim(norm_gain, own_start, share_cols, 0)
        normed_share = (values * inverse[:, None] * own_gain[None, :]).astype(jnp.bfloat16)
        normed = collect(normed_share, "tp", 1)
        picked, weighted = routing_tables(routes[step_index], route_weights[step_index], CAP)
        selected = jnp.einsum(
            "ecr,rd->ecd", picked, normed, preferred_element_type=jnp.float32
        ).astype(jnp.bfloat16)
        partial_value = local_experts(selected, weighted, restored)
        current = (
            mixed.astype(jnp.float32) + sent_and_summed(partial_value.astype(jnp.bfloat16), "tp", 1)
        ).astype(jnp.bfloat16)
    return (current, scale_log2)


def solution(mesh):
    in_specs = (
        P("fsdp", None),
        P(None, ("fsdp", "tp"), None),
        P(("fsdp", "tp"), None, None),
        P(("fsdp", "tp"), None, None),
        P(None, ("fsdp", "tp"), None),
        P(None, ("fsdp", "tp"), None),
        P(("fsdp", "tp")),
        P(None, "fsdp", None),
        P(None, "fsdp", None),
        P(),
        P(None, ("fsdp", "tp"), None),
        P(None, ("fsdp", "tp"), None),
        P(None, ("fsdp", "tp"), None),
        P("tp", None),
    )
    out_specs = (P("fsdp", "tp"), P())
    return jax.shard_map(local, mesh=mesh, in_specs=in_specs, out_specs=out_specs, check_vma=False)
```

profile of v0, /device:TPU:0, one launch (start us, length us, event | category | flops | bytes accessed | tf_op | source)
XLA Modules:
  0.0 576.3 jit_solution(13156694128293218370)
XLA Ops:
  11.7 69.4 %pmax.7 = f32[3,8,12,32]{3,2,1,0:T(8,128)S(1)} all-reduce(f32[3,8,12,32]{3,2,1,0:T(8,128)S(1)} %copy.88), channel_id=1, replica_groups=mesh['fsdp'=16,'tp'=8] {'fsdp','tp'}, use_global_device_ids=true, to_apply=%region_11.12 | all-reduce | flops 9216 | bytes 73728 | tf_op jit(solution)/shard_map/pmax | solution.py:177
  81.6 7.7 %multiply_convert_fusion = bf16[3,8,12,4096]{3,1,2,0:T(8,128)(2,1)} fusion(f32[1,8,12,4096]{3,1,2,0:T(8,128)} %bitcast.173, f32[1,8,12,4096]{3,1,2,0:T(8,128)} %bitcast.175, f32[1,8,12,4096]{3,1,2,0:T(8,128)} %bitcast.177, f32[3,8,12,32]{1,3,2,0:T(8,128)S(1)} %copy.89), kind=kLoop, calls=%fused_computation.6 | loop fusion | flops 20054016 | bytes 7114752 | tf_op jit(solution)/shard_map/convert_element_type | solution.py:184
  100.4 4.2 all-to-all-done
  104.6 5.2 convolution_convert_fusion.3
  117.9 7.5 %all-to-all-done.1 = bf16[8,64,512]{2,1,0:T(8,128)(2,1)S(1)} async-done(((bf16[8,64,512]{2,1,0:T(8,128)(2,1)}), bf16[8,64,512]{2,1,0:T(8,128)(2,1)S(1)}, u32[]{:S(2)}, u32[]{:S(2)}) %all-to-all-start.1) | async-done | bytes 524320 | tf_op jit(solution)/shard_map/all_to_all | solution.py:30
  129.9 24.9 %psum.14 = f32[64]{0:T(128)S(1)} all-reduce(f32[64]{0:T(128)S(1)} %get-tuple-element.16), channel_id=1, replica_groups=mesh['fsdp'=16,'tp'=8] {'tp'}, use_global_device_ids=true, to_apply=%region_8.9 | all-reduce | flops 64 | bytes 512 | tf_op jit(solution)/shard_map/psum | solution.py:207
  159.3 5.0 convolution_convert_fusion.1
  169.0 3.9 all-to-all-start.5
  173.8 122.2 %all-gather.2.cloned.1.call-done = bf16[3,8,192,4096]{3,1,2,0:T(8,128)(2,1)} async-done(((bf16[3,8,12,4096]{3,1,2,0:T(8,128)(2,1)}), bf16[3,8,192,4096]{3,1,2,0:T(8,128)(2,1)}) %all-gather.2.cloned.1.call-update) | async-done | bytes 37748752 | tf_op jit(solution)/shard_map/all_gather | solution.py:187
  296.0 36.6 %bitcast_convert_fusion = f32[3,8,192,32,128]{4,1,3,2,0:T(8,128)} fusion(bf16[3,8,192,4096]{3,1,2,0:T(8,128)(2,1)} %all-gather.2.cloned.1.call-done), kind=kLoop, calls=%fused_computation.2 | loop fusion | flops 18874368 | bytes 113246208 | tf_op jit(solution)/shard_map/reshape | solution.py:76
  332.7 38.8 %fusion = bf16[3,8,192,32,128]{4,3,2,1,0:T(8,128)(2,1)} fusion(f32[3,8,192,32,128]{4,1,3,2,0:T(8,128)} %bitcast_convert_fusion, f32[3,8,192,32]{3,2,1,0:T(8,128)} %copy.90), kind=kLoop, calls=%fused_computation.1 | loop fusion | flops 37748736 | bytes 113836032 | tf_op jit(solution)/shard_map/convert_element_type | solution.py:77
  371.5 25.3 %fusion.120 = (bf16[1,8,192,32,128]{4,3,2,1,0:T(8,128)(2,1)}, bf16[1,8,192,32,128]{4,3,2,1,0:T(8,128)(2,1)}, bf16[1,8,192,32,128]{4,3,2,1,0:T(8,128)(2,1)}) fusion(bf16[3,8,192,32,128]{4,3,2,1,0:T(8,128)(2,1)} %fusion), kind=kLoop, calls=%fused_computation.189 | loop fusion | bytes 75497472 | tf_op jit(solution)/shard_map/slice | solution.py:144
  396.8 19.3 %squeeze.16 = bf16[8,192,4096]{2,1,0:T(8,128)(2,1)} reshape(bf16[1,8,192,32,128]{4,3,2,1,0:T(8,128)(2,1)} %get-tuple-element.19) | data formatting | bytes 25165824 | tf_op jit(solution)/shard_map/squeeze | solution.py:144
  416.1 19.3 %squeeze.7 = bf16[8,192,4096]{2,1,0:T(8,128)(2,1)} reshape(bf16[1,8,192,32,128]{4,3,2,1,0:T(8,128)(2,1)} %get-tuple-element.20) | data formatting | bytes 25165824 | tf_op jit(solution)/shard_map/squeeze | solution.py:144
  435.4 19.3 %squeeze.6 = bf16[8,192,4096]{2,1,0:T(8,128)(2,1)} reshape(bf16[1,8,192,32,128]{4,3,2,1,0:T(8,128)(2,1)} %get-tuple-element.18) | data formatting | bytes 25165824 | tf_op jit(solution)/shard_map/squeeze | solution.py:144
  454.7 7.9 %fusion.122 = f32[8,8,192]{2,1,0:T(8,128)S(1)} fusion(bf16[8,8,4096]{2,1,0:T(8,128)(2,1)S(1)} %convolution_convert_fusion.2, bf16[8,192,4096]{2,1,0:T(8,128)(2,1)} %squeeze.6), kind=kOutput, calls=%fused_computation.191 | convolution fusion | flops 100663296 | bytes 13156352 | tf_op jit(solution)/shard_map/ecd,ehd->ech/dot_general | solution.py:137
  462.6 10.7 %fusion.39 = f32[8,8,4096]{2,1,0:T(8,128)S(1)} fusion(bf16[8,192,4096]{2,1,0:T(8,128)(2,1)} %squeeze.16, bf16[8,8,4096]{2,1,0:T(8,128)(2,1)S(1)} %convolution_convert_fusion.2, bf16[8,192,4096]{2,1,0:T(8,128)(2,1)} %squeeze.7, f32[8,8,192]{2,1,0:T(8,128)S(1)} %fusion.122), kind=kOutput, calls=%fused_computation.48 | convolution fusion | flops 201400320 | bytes 26787840 | tf_op jit(solution)/shard_map/ech,ehd->ecd/dot_general | solution.py:140
  475.8 6.4 %all-to-all-start.3 = ((bf16[8,64,512]{2,1,0:T(8,128)(2,1)}), bf16[8,64,512]{2,1,0:T(8,128)(2,1)S(1)}, u32[]{:S(2)}, u32[]{:S(2)}) async-start(bf16[8,64,512]{2,1,0:T(8,128)(2,1)} %bitcast.169), calls=%async_computation.3 | async-start | bytes 1048576 | tf_op jit(solution)/shard_map/all_to_all | solution.py:30
  482.5 11.0 %all-to-all-done.3 = bf16[8,64,512]{2,1,0:T(8,128)(2,1)S(1)} async-done(((bf16[8,64,512]{2,1,0:T(8,128)(2,1)}), bf16[8,64,512]{2,1,0:T(8,128)(2,1)S(1)}, u32[]{:S(2)}, u32[]{:S(2)}) %all-to-all-start.3) | async-done | bytes 524320 | tf_op jit(solution)/shard_map/all_to_all | solution.py:30
  493.7 21.1 %psum.15 = f32[64]{0:T(128)S(1)} all-reduce(f32[64]{0:T(128)S(1)} %get-tuple-element.14), channel_id=1, replica_groups=mesh['fsdp'=16,'tp'=8] {'tp'}, use_global_device_ids=true, to_apply=%region_23.24 | all-reduce | flops 64 | bytes 512 | tf_op jit(solution)/shard_map/psum | solution.py:207
  519.6 9.3 %all-to-all-done.6 = bf16[8,64,512]{2,1,0:T(8,128)(2,1)S(1)} async-done(((bf16[8,64,512]{2,1,0:T(8,128)(2,1)}), bf16[8,64,512]{2,1,0:T(8,128)(2,1)S(1)}, u32[]{:S(2)}, u32[]{:S(2)}) %all-to-all-start.6) | async-done | bytes 524320 | tf_op jit(solution)/shard_map/all_to_all | solution.py:36
  529.7 7.9 %fusion.123 = f32[8,8,192]{2,1,0:T(8,128)S(1)} fusion(bf16[8,8,4096]{2,1,0:T(8,128)(2,1)S(1)} %convolution_convert_fusion, bf16[8,192,4096]{2,1,0:T(8,128)(2,1)} %squeeze.6), kind=kOutput, calls=%fused_computation.192 | convolution fusion | flops 100663296 | bytes 13156352 | tf_op jit(solution)/shard_map/ecd,ehd->ech/dot_general | solution.py:137
  537.7 14.4 %fusion.38 = f32[8,8,4096]{2,1,0:T(8,128)} fusion(bf16[8,192,4096]{2,1,0:T(8,128)(2,1)} %squeeze.16, bf16[8,8,4096]{2,1,0:T(8,128)(2,1)S(1)} %convolution_convert_fusion, bf16[8,192,4096]{2,1,0:T(8,128)(2,1)} %squeeze.7, f32[8,8,192]{2,1,0:T(8,128)S(1)} %fusion.123), kind=kOutput, calls=%fused_computation.47 | convolution fusion | flops 201400320 | bytes 26787840 | tf_op jit(solution)/shard_map/ech,ehd->ecd/dot_general | solution.py:140
  559.9 8.8 %all-to-all-done.7 = bf16[8,64,512]{2,1,0:T(8,128)(2,1)S(1)} async-done(((bf16[8,64,512]{2,1,0:T(8,128)(2,1)}), bf16[8,64,512]{2,1,0:T(8,128)(2,1)S(1)}, u32[]{:S(2)}, u32[]{:S(2)}) %all-to-all-start.7) | async-done | bytes 524320 | tf_op jit(solution)/shard_map/all_to_all | solution.py:30
  (107 shorter events, 55.4 us)
Async XLA Ops:
  7.2 82.6 %copy-start = (bf16[8,256,512]{2,1,0:T(8,128)(2,1)S(1)}, bf16[8,256,512]{2,1,0:T(8,128)(2,1)}, u32[]{:S(2)}) copy-start(bf16[8,256,512]{2,1,0:T(8,128)(2,1)} %param.16) | copy-start | bytes 6291460
  7.2 288.8 %all-gather.2.cloned.1.call-start = ((), (), s32[]{:S(2)}) async-start(), calls=%async_computation.8 | async-start | bytes 40108032 | tf_op jit(solution)/shard_map/all_gather | solution.py:187
  81.6 7.8 %copy-start.2 = (bf16[2,8,8192]{2,1,0:T(8,128)(2,1)S(1)}, bf16[2,8,8192]{2,1,0:T(8,128)(2,1)}, u32[]{:S(2)}) copy-start(bf16[2,8,8192]{2,1,0:T(8,128)(2,1)} %param.15) | copy-start | bytes 786436
  81.6 7.9 %copy-start.5 = (bf16[2,8,512]{2,1,0:T(8,128)(2,1)S(1)}, bf16[2,8,512]{2,1,0:T(8,128)(2,1)}, u32[]{:S(2)}) copy-start(bf16[2,8,512]{2,1,0:T(8,128)(2,1)} %param.19) | copy-start | bytes 49156
  81.6 7.9 %copy-start.7 = (s32[8]{0:T(128)S(1)}, s32[8]{0:T(128)}, u32[]{:S(2)}) copy-start(s32[8]{0:T(128)} %param.20) | copy-start | bytes 100
  81.6 8.0 %copy-start.6 = (bf16[2,8,512]{2,1,0:T(8,128)(2,1)S(1)}, bf16[2,8,512]{2,1,0:T(8,128)(2,1)}, u32[]{:S(2)}) copy-start(bf16[2,8,512]{2,1,0:T(8,128)(2,1)} %param.18) | copy-start | bytes 49156
  89.4 2.0 copy-start.8
  90.5 6.0 %copy-start.3 = (s32[2,64,8]{1,2,0:T(8,128)S(1)}, s32[2,64,8]{1,2,0:T(8,128)}, u32[]{:S(2)}) copy-start(s32[2,64,8]{1,2,0:T(8,128)} %param.21) | copy-start | bytes 12292
  91.9 8.5 %copy-start.4 = (f32[2,64,8]{1,2,0:T(8,128)S(1)}, f32[2,64,8]{1,2,0:T(8,128)}, u32[]{:S(2)}) copy-start(f32[2,64,8]{1,2,0:T(8,128)} %param.22) | copy-start | bytes 12292
  92.7 11.9 %all-to-all-start = ((bf16[8,8,1024]{2,0,1:T(8,128)(2,1)}), bf16[8,8,1024]{2,0,1:T(8,128)(2,1)S(1)}, u32[]{:S(2)}, u32[]{:S(2)}) async-start(bf16[8,8,1024]{2,0,1:T(8,128)(2,1)} %copy.83), calls=%async_computation | async-start | bytes 262144 | tf_op jit(solution)/shard_map/all_to_all | solution.py:201
  110.7 14.8 %all-to-all-start.1 = ((bf16[8,64,512]{2,1,0:T(8,128)(2,1)}), bf16[8,64,512]{2,1,0:T(8,128)(2,1)S(1)}, u32[]{:S(2)}, u32[]{:S(2)}) async-start(bf16[8,64,512]{2,1,0:T(8,128)(2,1)} %bitcast.171), calls=%async_computation.1 | async-start | bytes 1048576 | tf_op jit(solution)/shard_map/all_to_all | solution.py:30
  125.5 29.5 %all-to-all-start.4 = ((bf16[8,8,1024]{2,0,1:T(8,128)(2,1)}), bf16[8,8,1024]{2,0,1:T(8,128)(2,1)S(1)}, u32[]{:S(2)}, u32[]{:S(2)}) async-start(bf16[8,8,1024]{2,0,1:T(8,128)(2,1)} %copy.98), calls=%async_computation.4 | async-start | bytes 262144 | tf_op jit(solution)/shard_map/all_to_all | solution.py:201
  155.8 13.2 %all-to-all-start.2 = ((bf16[8,64,512]{2,1,0:T(8,128)(2,1)}), bf16[8,64,512]{2,1,0:T(8,128)(2,1)S(1)}, u32[]{:S(2)}, u32[]{:S(2)}) async-start(bf16[8,64,512]{2,1,0:T(8,128)(2,1)} %broadcast_in_dim.124), calls=%async_computation.2 | async-start | bytes 1048576 | tf_op jit(solution)/shard_map/all_to_all | solution.py:36
  169.0 306.8 %all-to-all-start.5 = ((bf16[8,64,512]{2,1,0:T(8,128)(2,1)}), bf16[8,64,512]{2,1,0:T(8,128)(2,1)S(1)}, u32[]{:S(2)}, u32[]{:S(2)}) async-start(bf16[8,64,512]{2,1,0:T(8,128)(2,1)} %bitcast.167), calls=%async_computation.5 | async-start | bytes 1048576 | tf_op jit(solution)/shard_map/all_to_all | solution.py:30
  475.8 17.7 %all-to-all-start.3 = ((bf16[8,64,512]{2,1,0:T(8,128)(2,1)}), bf16[8,64,512]{2,1,0:T(8,128)(2,1)S(1)}, u32[]{:S(2)}, u32[]{:S(2)}) async-start(bf16[8,64,512]{2,1,0:T(8,128)(2,1)} %bitcast.169), calls=%async_computation.3 | async-start | bytes 1048576 | tf_op jit(solution)/shard_map/all_to_all | solution.py:30
  515.8 13.1 %all-to-all-start.6 = ((bf16[8,64,512]{2,1,0:T(8,128)(2,1)}), bf16[8,64,512]{2,1,0:T(8,128)(2,1)S(1)}, u32[]{:S(2)}, u32[]{:S(2)}) async-start(bf16[8,64,512]{2,1,0:T(8,128)(2,1)} %broadcast_in_dim.130), calls=%async_computation.6 | async-start | bytes 1048576 | tf_op jit(solution)/shard_map/all_to_all | solution.py:36
  537.6 31.8 %copy-start.1 = (bf16[8,256,512]{2,1,0:T(8,128)(2,1)S(1)}, bf16[8,256,512]{2,1,0:T(8,128)(2,1)}, u32[]{:S(2)}) copy-start(bf16[8,256,512]{2,1,0:T(8,128)(2,1)} %param.16) | copy-start | bytes 6291460
  555.7 13.1 %all-to-all-start.7 = ((bf16[8,64,512]{2,1,0:T(8,128)(2,1)}), bf16[8,64,512]{2,1,0:T(8,128)(2,1)S(1)}, u32[]{:S(2)}, u32[]{:S(2)}) async-start(bf16[8,64,512]{2,1,0:T(8,128)(2,1)} %bitcast.165), calls=%async_computation.7 | async-start | bytes 1048576 | tf_op jit(solution)/shard_map/all_to_all | solution.py:30
Sparse Core Ops, SparseCore 0:
  89.5 206.4 all-gather.1
where the time goes:
time: 579 us; the launch traced here: 576 us
  waiting for transfers between devices  167 us (29%)
  blocking collectives  115 us (20%)
  local copies, waits for them, and re-layouts  95.3 us (16%)
  other arithmetic  90.6 us (16%)
  matrix products  61.6 us (11%)
  starting transfers between devices  31.9 us (6%)
  between operations  14.5 us (3%)
    all_gather x1, waiting for transfers between devices, local(): gathered = lax.all_gather(quantized, 'fsdp', axis=2, tiled=True)  122 us
    pmax x1, blocking collectives, local(): block_max = lax.pmax(partial_max, ('fsdp', 'tp'))  69.4 us
    squeeze x3, local copies, waits for them, and re-layouts, local_experts(): outputs = expert_rows(selected, restored[0], restored[1], restored[2])  57.9 us
    psum x2, blocking collectives, local(): squares = lax.psum(jnp.sum(values * values, axis=1), 'tp')  46.1 us
    convert_element_type x1, other arithmetic, dequantize(): (tiles * factors[..., None]).astype(jnp.bfloat16).reshape(3, WIN, count, D)  38.8 us
    reshape x1, other arithmetic, dequantize(): shard_piece.astype(jnp.float32).reshape(3, WIN, count, D // BLOCK, BLOCK)  36.6 us
    all_to_all x4, waiting for transfers between devices, sent_and_summed(): lax.all_to_all(blocks, axis, split_axis=0, concat_axis=0, tiled=True)  27.3 us
    slice x1, local copies, waits for them, and re-layouts, local_experts(): outputs = expert_rows(selected, restored[0], restored[1], restored[2])  25.3 us
  transfers between devices with their start and end apart: 9, of which 7 were waited for; matrix products, arithmetic and copies ran while one was open for 36% of the time, Pallas kernels for 0%

commit v1 on v0

v1 whole, which is shorter than its diff:
```python
import jax
import jax.numpy as jnp
from jax import lax
from jax.sharding import PartitionSpec as P

D = 4096
FF = 1536
QH = 64
KVH = 4
HD = 128
BLOCK = 128
WIN = 8
CAP = 8


neg_fill = -1e30
epsilon = 1e-06
fp_limit = 448.0
grid_floor = 2.0 ** (-10)
least_exponent = -6.0


def cut_along(array, dim, peers):
    before, after = (array.shape[:dim], array.shape[dim + 1 :])
    return jnp.moveaxis(array.reshape(*before, peers, -1, *after), dim, 0)


def sent_and_summed(array, axis, dim):
    blocks = cut_along(array, dim, lax.axis_size(axis))
    arrived = lax.all_to_all(blocks, axis, split_axis=0, concat_axis=0, tiled=True)
    return arrived.astype(jnp.float32).sum(axis=0)


def copy_for_each(array, axis):
    peers = lax.axis_size(axis)
    return lax.all_to_all(
        jnp.broadcast_to(array[None], (peers, *array.shape)), axis, 0, 0, tiled=True
    )


def joined_along(blocks, dim):
    blocks = jnp.moveaxis(blocks, 0, dim)
    lengths = blocks.shape
    return blocks.reshape(*lengths[:dim], lengths[dim] * lengths[dim + 1], *lengths[dim + 2 :])


def collect(array, axis, dim):
    blocks = copy_for_each(array, axis)
    return joined_along(blocks, dim)


def grid_round(values):
    magnitude = jnp.abs(values)
    exponent = jnp.maximum(jnp.floor(jnp.log2(jnp.maximum(magnitude, grid_floor))), least_exponent)
    spacing = jnp.exp2(exponent - 3.0)
    return jnp.sign(values) * jnp.floor(magnitude / spacing + 0.5) * spacing


def attention_rows(queries_now, cache_keys, cache_values, fresh_keys, fresh_values, lengths):
    row_count = queries_now.shape[0]
    positions = cache_keys.shape[1]
    group = QH // KVH
    score_scale = HD ** (-0.5)
    fresh_count = fresh_keys.shape[0]
    query_heads = queries_now.reshape(row_count, KVH, group, HD)
    key_heads = cache_keys.reshape(row_count, positions, KVH, HD)
    value_heads = cache_values.reshape(row_count, positions, KVH, HD)
    fresh_key_heads = fresh_keys.reshape(fresh_count, row_count, KVH, HD)
    fresh_value_heads = fresh_values.reshape(fresh_count, row_count, KVH, HD)
    cached_scores = (
        jnp.einsum("rkgd,rpkd->rkgp", query_heads, key_heads, preferred_element_type=jnp.float32)
        * score_scale
    )
    fresh_scores = (
        jnp.einsum(
            "rkgd,srkd->rkgs", query_heads, fresh_key_heads, preferred_element_type=jnp.float32
        )
        * score_scale
    )
    alive_mask = (jnp.arange(positions, dtype=jnp.int32)[None, :] < lengths[:, None])[
        :, None, None, :
    ]
    peak_score = jnp.maximum(
        jnp.max(jnp.where(alive_mask, cached_scores, neg_fill), axis=-1),
        jnp.max(fresh_scores, axis=-1),
    )
    cached_weights = jnp.where(alive_mask, jnp.exp(cached_scores - peak_score[..., None]), 0.0)
    fresh_weights = jnp.exp(fresh_scores - peak_score[..., None])
    weight_sum = jnp.sum(cached_weights, axis=-1) + jnp.sum(fresh_weights, axis=-1)
    cached_probs = (cached_weights / weight_sum[..., None]).astype(jnp.bfloat16)
    fresh_probs = (fresh_weights / weight_sum[..., None]).astype(jnp.bfloat16)
    output = jnp.einsum(
        "rkgp,rpkd->rkgd", cached_probs, value_heads, preferred_element_type=jnp.float32
    )
    output = output + jnp.einsum(
        "rkgs,srkd->rkgd", fresh_probs, fresh_value_heads, preferred_element_type=jnp.float32
    )
    return output.astype(jnp.bfloat16).reshape(row_count, QH * HD)


def routing_tables(routes, route_weights):
    rows = routes.shape[0]
    weight_sum = jnp.sum(route_weights, axis=1)
    experts = jnp.arange(WIN, dtype=jnp.int32)
    matches = routes[None, :, :] == experts[:, None, None]
    chosen = jnp.any(matches, axis=2)
    gate_share = (
        jnp.sum(jnp.where(matches, route_weights[None, :, :], 0.0), axis=2) / weight_sum[None, :]
    )
    earlier = jnp.arange(rows)[:, None] < jnp.arange(rows)[None, :]
    slot_index = jnp.sum(jnp.where(earlier[None], chosen.astype(jnp.int32)[:, :, None], 0), axis=1)
    places = jnp.arange(CAP, dtype=jnp.int32)
    picked = (slot_index[:, None, :] == places[None, :, None]) & chosen[:, None, :]
    slot_share = jnp.sum(jnp.where(picked, gate_share[:, None, :], 0.0), axis=2)
    return (picked.astype(jnp.bfloat16), slot_share)


def block_maxima(masters, fsdp_pos, tp_pos, tp_count):
    shard_rows = masters.shape[2]
    magnitude = jnp.max(jnp.abs(masters).reshape(3, WIN, shard_rows, D // BLOCK, BLOCK), axis=4)
    first_tile = (fsdp_pos * shard_rows * tp_count) // BLOCK
    owned = (fsdp_pos * tp_count + tp_pos) * shard_rows + jnp.arange(shard_rows, dtype=jnp.int32)
    second = (owned // BLOCK - first_tile) == 1
    mine = jnp.stack(
        [
            jnp.max(jnp.where(second[None, None, :, None], 0.0, magnitude), axis=2),
            jnp.max(jnp.where(second[None, None, :, None], magnitude, 0.0), axis=2),
        ]
    )
    group = jnp.max(copy_for_each(mine, "tp"), axis=0)
    every = copy_for_each(group, "fsdp")
    tiles = []
    for tile in range(FF // BLOCK):
        parts = []
        for owner in range(16):
            first = owner * 96 // BLOCK
            if first == tile:
                parts.append(every[owner, 0])
            if first + 1 == tile and owner * 96 + 95 >= tile * BLOCK:
                parts.append(every[owner, 1])
        tiles.append(jnp.max(jnp.stack(parts), axis=0))
    return jnp.stack(tiles, axis=2), first_tile, second


def local(
    hidden_in,
    queries,
    key_cache,
    value_cache,
    new_keys,
    new_values,
    lengths,
    routes,
    route_weights,
    norm_gain,
    gate_master,
    up_master,
    down_master,
    out_proj,
):
    tp_count = lax.axis_size("tp")
    fsdp_pos = lax.axis_index("fsdp")
    tp_pos = lax.axis_index("tp")
    shard_rows = gate_master.shape[1]
    masters = jnp.stack([gate_master, up_master, down_master])
    block_max, first_tile, second = block_maxima(masters, fsdp_pos, tp_pos, tp_count)
    scales = (block_max + epsilon) / fp_limit
    scale_log2 = jnp.log2(scales)
    near = lax.dynamic_slice_in_dim(scales, first_tile, 1, 2)
    far = lax.dynamic_slice_in_dim(scales, jnp.minimum(first_tile + 1, FF // BLOCK - 1), 1, 2)
    factors = jnp.where(second[None, None, :, None], far, near)[..., None]
    tiles = masters.reshape(3, WIN, shard_rows, D // BLOCK, BLOCK)
    quantized = grid_round(tiles / factors).astype(jnp.bfloat16).astype(jnp.float32)
    restored = (quantized * factors).astype(jnp.bfloat16).reshape(3, WIN, shard_rows, D)
    arrived = lax.all_to_all(
        restored.transpose(1, 0, 2, 3), "tp", split_axis=0, concat_axis=0, tiled=True
    )
    own = [arrived[:, i].reshape(tp_count * shard_rows, D) for i in range(3)]

    share_cols = D // tp_count
    own_start = tp_pos * share_cols
    current = lax.dynamic_slice_in_dim(hidden_in, own_start, share_cols, 1)
    tables = [routing_tables(routes[s], route_weights[s]) for s in range(2)]
    heads = jnp.stack(
        [
            attention_rows(
                queries[s], key_cache, value_cache, new_keys[: s + 1], new_values[: s + 1], lengths
            )
            for s in range(2)
        ]
    )
    regrouped = lax.all_to_all(heads, "tp", split_axis=2, concat_axis=1, tiled=True)
    projections = []
    for s in range(2):
        projected = jnp.dot(regrouped[s], out_proj, preferred_element_type=jnp.float32)
        projections.append(projected.astype(jnp.bfloat16))
    both = jnp.stack(projections)
    summed = sent_and_summed(both, "tp", 2)
    for s in range(2):
        picked, slot_share = tables[s]
        mixed = (current.astype(jnp.float32) + summed[s]).astype(jnp.bfloat16)
        slots = picked.reshape(WIN * CAP, -1)
        chosen = jnp.dot(slots, mixed, preferred_element_type=jnp.float32).astype(jnp.bfloat16)
        rows = collect_slots(chosen)
        values = rows.astype(jnp.float32)
        inverse = lax.rsqrt(jnp.mean(values * values, axis=1, keepdims=True) + epsilon)
        normed = (values * inverse * norm_gain[None, :]).astype(jnp.bfloat16)
        everyone = copy_for_each(normed, "fsdp").reshape(-1, D)
        gate = jnp.einsum("rd,hd->rh", everyone, own[0], preferred_element_type=jnp.float32)
        up = jnp.einsum("rd,hd->rh", everyone, own[1], preferred_element_type=jnp.float32)
        act = (jax.nn.silu(gate) * up).astype(jnp.bfloat16)
        partial = jnp.dot(act, own[2], preferred_element_type=jnp.float32).astype(jnp.bfloat16)
        output = sent_and_summed(partial, "fsdp", 0)
        share = lax.dynamic_slice_in_dim(slot_share, tp_pos, 1, 0)[0]
        weighted = (output * share[:, None]).astype(jnp.bfloat16)
        returned = lax.all_to_all(
            cut_along(weighted, 1, tp_count), "tp", split_axis=0, concat_axis=0, tiled=True
        ).reshape(WIN * CAP, share_cols)
        moe = lax.dot_general(
            slots, returned, (((0,), (0,)), ((), ())), preferred_element_type=jnp.float32
        )
        current = (mixed.astype(jnp.float32) + moe).astype(jnp.bfloat16)
    return (current, scale_log2)


def collect_slots(chosen):
    arrived = lax.all_to_all(chosen, "tp", split_axis=0, concat_axis=0, tiled=True)
    blocks = arrived.reshape(-1, CAP, chosen.shape[1])
    return joined_along(blocks, 1)


def solution(mesh):
    in_specs = (
        P("fsdp", None),
        P(None, ("fsdp", "tp"), None),
        P(("fsdp", "tp"), None, None),
        P(("fsdp", "tp"), None, None),
        P(None, ("fsdp", "tp"), None),
        P(None, ("fsdp", "tp"), None),
        P(("fsdp", "tp")),
        P(None, "fsdp", None),
        P(None, "fsdp", None),
        P(),
        P(None, ("fsdp", "tp"), None),
        P(None, ("fsdp", "tp"), None),
        P(None, ("fsdp", "tp"), None),
        P("tp", None),
    )
    out_specs = (P("fsdp", "tp"), P())
    return jax.shard_map(local, mesh=mesh, in_specs=in_specs, out_specs=out_specs, check_vma=False)
```

time: 579 us -> 297 us (0.51)
  blocking collectives: 115 us -> 39.5 us
  other arithmetic: 90.6 us -> 17 us
  waiting for transfers between devices: 167 us -> 111 us
  local copies, waits for them, and re-layouts: 95.3 us -> 51.2 us
  matrix products: 61.6 us -> 26.1 us
  starting transfers between devices: 31.9 us -> 49.5 us
  between operations: 14.5 us -> 1.34 us
    all_gather x1 -> x0, waiting for transfers between devices: 122 us -> none  [local(): gathered = lax.all_gather(quantized, 'fsdp', axis=2, tiled=True)]
    pmax x1 -> x0, blocking collectives: 69.4 us -> none  [local(): block_max = lax.pmax(partial_max, ('fsdp', 'tp'))]
    squeeze x3 -> x0, local copies, waits for them, and re-layouts: 57.9 us -> none  [local_experts(): outputs = expert_rows(selected, restored[0], restored[1], restored[2])]
    all_to_all x2 -> x4, waiting for transfers between devices: 4.25 us -> 58.8 us  [the longest x1 44.2 us: local(): lax.all_to_all(restored.transpose(1, 0, 2, 3), 'tp', split_axis=0, concat...]
    convert_element_type x7, other arithmetic: 47.3 us -> 1.06 us  [the longest x1 0.86 us: local(): mixed = (current.astype(jnp.float32) + summed[s]).astype(jnp.bfloat16)]
    psum x2 -> x0, blocking collectives: 46.1 us -> none  [local(): squares = lax.psum(jnp.sum(values * values, axis=1), 'tp')]
    all_to_all x0 -> x3, blocking collectives: none -> 39.5 us  [the longest x1 19.1 us: copy_for_each(): lax.all_to_all(jnp.broadcast_to(array[None], (peers, *array.shape)), axis...]
    reshape x1 -> x0, other arithmetic: 36.6 us -> none  [dequantize(): shard_piece.astype(jnp.float32).reshape(3, WIN, count, D // BLOCK, BLOCK)]
  transfers between devices with their start and end apart: 9 -> 10, of which waited for: 7 -> 8; matrix products, arithmetic and copies ran while one was open for 36% -> 16% of each run, Pallas kernels for 0% -> 0%
where the time goes in v1:
time: 297 us; the launch traced here: 296 us
  waiting for transfers between devices  111 us (37%)
  local copies, waits for them, and re-layouts  51.2 us (17%)
  starting transfers between devices  49.5 us (17%)
  blocking collectives  39.5 us (13%)
  matrix products  26.1 us (9%)
  other arithmetic  17 us (6%)
    all_to_all x1, waiting for transfers between devices, local(): lax.all_to_all(restored.transpose(1, 0, 2, 3), 'tp', split_axis=0, concat...  44.2 us
    all_to_all x3, waiting for transfers between devices, sent_and_summed(): lax.all_to_all(blocks, axis, split_axis=0, concat_axis=0, tiled=True)  37.5 us
    all_to_all x1, blocking collectives, copy_for_each(): lax.all_to_all(jnp.broadcast_to(array[None], (peers, *array.shape)), axis...  19.1 us
    all_to_all x3, starting transfers between devices, copy_for_each(): lax.all_to_all(jnp.broadcast_to(array[None], (peers, *array.shape)), axis...  16.2 us
    unnamed x38, local copies, waits for them, and re-layouts  15.3 us
    all_to_all x3, waiting for transfers between devices, copy_for_each(): lax.all_to_all(jnp.broadcast_to(array[None], (peers, *array.shape)), axis...  14.8 us
    all_to_all x3, starting transfers between devices, sent_and_summed(): lax.all_to_all(blocks, axis, split_axis=0, concat_axis=0, tiled=True)  11 us
    all_to_all x1, blocking collectives, collect_slots(): lax.all_to_all(chosen, 'tp', split_axis=0, concat_axis=0, tiled=True)  10.3 us
  transfers between devices with their start and end apart: 10, of which 8 were waited for; matrix products, arithmetic and copies ran while one was open for 16% of the time, Pallas kernels for 0%

profile of v1, /device:TPU:0, one launch (start us, length us, event | category | flops | bytes accessed | tf_op | source)
XLA Modules:
  0.0 295.8 jit_solution(17559378506708630502)
XLA Ops:
  0.7 3.8 %fusion = f32[3,8,12,32]{1,3,2,0:T(8,128)S(1)} fusion(f32[1,8,12,32,128]{4,1,3,2,0:T(8,128)} %bitcast.259, f32[1,8,12,32,128]{4,1,3,2,0:T(8,128)} %bitcast.261, f32[1,8,12,32,128]{4,1,3,2,0:T(8,128)} %bitcast.263), kind=kLoop, calls=%fused_computation.4 | loop fusion | flops 4709376 | bytes 4755456 | tf_op jit(solution)/shard_map/reduce_max | solution.py:120
  5.7 7.0 %all-to-all-start.4 = ((f32[8,1,1536]{2,1,0:T(1,128)}), f32[8,1,1536]{2,1,0:T(1,128)S(1)}, u32[]{:S(2)}, u32[]{:S(2)}) async-start(f32[8,1,1536]{2,1,0:T(1,128)} %reshape.598), calls=%async_computation.4 | async-start | bytes 98304 | tf_op jit(solution)/shard_map/all_to_all | solution.py:36
  18.4 6.7 %copy.154 = bf16[2,8,8192]{1,0,2:T(2,128)(2,1)} copy(bf16[2,8,8192]{2,1,0:T(8,128)(2,1)S(1)} %pad_maximum_fusion) | data formatting | bytes 524288 | tf_op jit(solution)/shard_map/stack | solution.py:184
  25.1 6.4 %reshape.602 = bf16[8,2,8192]{2,1,0:T(2,128)(2,1)} reshape(bf16[8192,2,8]{2,1,0:T(2,128)(2,1)} %bitcast.257) | data formatting | bytes 524288
  33.9 5.5 %all-to-all-start.5 = ((f32[16,1,1536]{2,1,0:T(1,128)}), f32[16,1,1536]{2,1,0:T(1,128)S(1)}, u32[]{:S(2)}, u32[]{:S(2)}) async-start(f32[16,1,1536]{2,1,0:T(1,128)} %reshape.600), calls=%async_computation.5 | async-start | bytes 196608 | tf_op jit(solution)/shard_map/all_to_all | solution.py:36
  39.7 6.1 %all-to-all-done.5 = f32[16,1,1536]{2,1,0:T(1,128)S(1)} async-done(((f32[16,1,1536]{2,1,0:T(1,128)}), f32[16,1,1536]{2,1,0:T(1,128)S(1)}, u32[]{:S(2)}, u32[]{:S(2)}) %all-to-all-start.5) | async-done | bytes 98336 | tf_op jit(solution)/shard_map/all_to_all | solution.py:36
  45.8 7.8 %all-to-all-start = ((bf16[8,2,8192]{2,1,0:T(2,128)(2,1)}), bf16[8,2,8192]{2,1,0:T(2,128)(2,1)S(1)}, u32[]{:S(2)}, u32[]{:S(2)}) async-start(bf16[8,2,8192]{2,1,0:T(2,128)(2,1)} %reshape.602), calls=%async_computation | async-start | bytes 524288 | tf_op jit(solution)/shard_map/all_to_all | solution.py:192
  54.7 7.6 %all-to-all-done = bf16[8,2,8192]{2,1,0:T(2,128)(2,1)S(1)} async-done(((bf16[8,2,8192]{2,1,0:T(2,128)(2,1)}), bf16[8,2,8192]{2,1,0:T(2,128)(2,1)S(1)}, u32[]{:S(2)}, u32[]{:S(2)}) %all-to-all-start) | async-done | bytes 262176 | tf_op jit(solution)/shard_map/all_to_all | solution.py:192
  62.4 5.9 %reshape.603 = bf16[8192,2,8]{2,1,0:T(2,128)(2,1)} reshape(bf16[8,2,8192]{2,1,0:T(2,128)(2,1)S(1)} %all-to-all-done) | data formatting | bytes 524288
  68.3 5.9 %copy.169 = bf16[2,8,8,1024]{3,2,1,0:T(8,128)(2,1)S(1)} copy(bf16[2,8,8,1024]{1,0,3,2:T(2,128)(2,1)} %bitcast.258) | data formatting | bytes 524288 | tf_op jit(solution)/shard_map/all_to_all | solution.py:192
  74.3 4.9 %convolution_convert_fusion.2 = bf16[64,4096]{1,0:T(8,128)(2,1)S(1)} fusion(bf16[1024,4096]{1,0:T(8,128)(2,1)} %param.27, bf16[1,8,8,1024]{3,1,2,0:T(8,128)(2,1)S(1)} %get-tuple-element.26), kind=kOutput, calls=%fused_computation.9 | convolution fusion | flops 537133056 | bytes 9043968 | tf_op jit(solution)/shard_map/dot_general | solution.py:195
  79.5 4.9 %convolution_convert_fusion.3 = bf16[64,4096]{1,0:T(8,128)(2,1)S(1)} fusion(bf16[1024,4096]{1,0:T(8,128)(2,1)} %param.27, bf16[1,8,8,1024]{3,1,2,0:T(8,128)(2,1)S(1)} %get-tuple-element.25), kind=kOutput, calls=%fused_computation.10 | convolution fusion | flops 537133056 | bytes 9043968 | tf_op jit(solution)/shard_map/dot_general | solution.py:195
  93.6 6.1 %div.124 = f32[3,8,12,4096]{3,1,2,0:T(8,128)} reshape(f32[3,8,12,32,128]{4,3,1,2,0:T(8,128)} %div.123) | data formatting | bytes 9437184 | tf_op jit(solution)/shard_map/div | solution.py:173
  99.7 4.7 %all-to-all-done.1 = bf16[8,2,64,512]{3,2,1,0:T(8,128)(2,1)S(1)} async-done(((bf16[8,2,64,512]{3,2,1,0:T(8,128)(2,1)}), bf16[8,2,64,512]{3,2,1,0:T(8,128)(2,1)S(1)}, u32[]{:S(2)}, u32[]{:S(2)}) %all-to-all-start.1) | async-done | bytes 1048608 | tf_op jit(solution)/shard_map/all_to_all | solution.py:30
  110.0 6.4 %fusion.3 = bf16[8,3,12,4096]{3,0,2,1:T(8,128)(2,1)S(1)} fusion(f32[3,8,12,4096]{3,1,2,0:T(8,128)} %div.124, f32[1,8,12,4096]{3,1,2,0:T(8,128)S(1)} %bitcast.260, f32[1,8,12,4096]{3,1,2,0:T(8,128)} %bitcast.262, f32[1,8,12,4096]{3,1,2,0:T(8,128)} %bitcast.264), kind=kLoop, calls=%fused_computation.11 | loop fusion | flops 23592960 | bytes 11796480 | tf_op jit(solution)/shard_map/transpose | solution.py:176
  119.5 7.3 %all-to-all-start.6 = ((bf16[8,3,12,4096]{3,2,1,0:T(8,128)(2,1)}), bf16[8,3,12,4096]{3,2,1,0:T(8,128)(2,1)}, u32[]{:S(2)}, u32[]{:S(2)}) async-start(bf16[8,3,12,4096]{3,2,1,0:T(8,128)(2,1)} %copy.165), calls=%async_computation.6 | async-start | bytes 6291456 | tf_op jit(solution)/shard_map/all_to_all | solution.py:175
  127.1 44.2 %all-to-all-done.6 = bf16[8,3,12,4096]{3,2,1,0:T(8,128)(2,1)} async-done(((bf16[8,3,12,4096]{3,2,1,0:T(8,128)(2,1)}), bf16[8,3,12,4096]{3,2,1,0:T(8,128)(2,1)}, u32[]{:S(2)}, u32[]{:S(2)}) %all-to-all-start.6) | async-done | bytes 2359328 | tf_op jit(solution)/shard_map/all_to_all | solution.py:175
  183.9 8.7 %all-to-all-done.3 = bf16[16,8,4096]{2,1,0:T(8,128)(2,1)S(1)} async-done(((bf16[16,8,4096]{2,1,0:T(8,128)(2,1)}), bf16[16,8,4096]{2,1,0:T(8,128)(2,1)S(1)}, u32[]{:S(2)}, u32[]{:S(2)}) %all-to-all-start.3) | async-done | bytes 1048608 | tf_op jit(solution)/shard_map/all_to_all | solution.py:36
  200.4 16.4 %all-to-all-done.7 = bf16[16,8,4096]{2,1,0:T(8,128)(2,1)S(1)} async-done(((bf16[16,8,4096]{2,1,0:T(8,128)(2,1)}), bf16[16,8,4096]{2,1,0:T(8,128)(2,1)S(1)}, u32[]{:S(2)}, u32[]{:S(2)}) %all-to-all-start.7) | async-done | bytes 1048608 | tf_op jit(solution)/shard_map/all_to_all | solution.py:30
  217.0 10.1 %all_to_all.83 = bf16[8,8,512]{2,1,0:T(8,128)(2,1)S(1)} all-to-all(bf16[8,8,512]{2,1,0:T(8,128)(2,1)S(1)} %fusion.69), channel_id=1, replica_groups=mesh['fsdp'=16,'tp'=8] {'tp'}, dimensions={0} | all-to-all | bytes 131072 | tf_op jit(solution)/shard_map/all_to_all | solution.py:216
  227.6 10.3 %all_to_all.84 = bf16[8,8,512]{2,1,0:T(8,128)(2,1)S(1)} all-to-all(bf16[8,8,512]{2,1,0:T(8,128)(2,1)S(1)} %fusion.42), channel_id=1, replica_groups=mesh['fsdp'=16,'tp'=8] {'tp'}, dimensions={0} | all-to-all | bytes 131072 | tf_op jit(solution)/shard_map/all_to_all | solution.py:227
  238.2 19.1 %all_to_all.85 = bf16[16,8,4096]{2,1,0:T(8,128)(2,1)S(1)} all-to-all(bf16[16,8,4096]{2,1,0:T(8,128)(2,1)S(1)} %broadcast_in_dim.230), channel_id=1, replica_groups=mesh['fsdp'=16,'tp'=8] {'fsdp'}, dimensions={0} | all-to-all | bytes 2097152 | tf_op jit(solution)/shard_map/all_to_all | solution.py:36
  266.6 16.4 %all-to-all-done.11 = bf16[16,8,4096]{2,1,0:T(8,128)(2,1)S(1)} async-done(((bf16[16,8,4096]{2,1,0:T(8,128)(2,1)}), bf16[16,8,4096]{2,1,0:T(8,128)(2,1)S(1)}, u32[]{:S(2)}, u32[]{:S(2)}) %all-to-all-start.11) | async-done | bytes 1048608 | tf_op jit(solution)/shard_map/all_to_all | solution.py:30
  287.9 7.0 %all-to-all-done.12 = bf16[8,8,512]{2,1,0:T(8,128)(2,1)S(1)} async-done(((bf16[8,8,512]{2,1,0:T(8,128)(2,1)}), bf16[8,8,512]{2,1,0:T(8,128)(2,1)S(1)}, u32[]{:S(2)}, u32[]{:S(2)}) %all-to-all-start.12) | async-done | bytes 65568 | tf_op jit(solution)/shard_map/all_to_all | solution.py:216
  (144 shorter events, 64.9 us)
Async XLA Ops:
  0.6 12.7 %copy-start = (bf16[8,256,512]{2,1,0:T(8,128)(2,1)S(1)}, bf16[8,256,512]{2,1,0:T(8,128)(2,1)}, u32[]{:S(2)}) copy-start(bf16[8,256,512]{2,1,0:T(8,128)(2,1)} %param.16) | copy-start | bytes 6291460
  0.6 12.0 %copy-start.5 = (bf16[2,8,8192]{2,1,0:T(8,128)(2,1)S(1)}, bf16[2,8,8192]{2,1,0:T(8,128)(2,1)}, u32[]{:S(2)}) copy-start(bf16[2,8,8192]{2,1,0:T(8,128)(2,1)} %param.15) | copy-start | bytes 786436
  0.7 12.1 %copy-start.11 = (s32[8]{0:T(128)S(1)}, s32[8]{0:T(128)}, u32[]{:S(2)}) copy-start(s32[8]{0:T(128)} %param.20) | copy-start | bytes 100
  0.7 12.2 %copy-start.10 = (bf16[2,8,512]{2,1,0:T(8,128)(2,1)S(1)}, bf16[2,8,512]{2,1,0:T(8,128)(2,1)}, u32[]{:S(2)}) copy-start(bf16[2,8,512]{2,1,0:T(8,128)(2,1)} %param.18) | copy-start | bytes 49156
  5.7 25.9 %all-to-all-start.4 = ((f32[8,1,1536]{2,1,0:T(1,128)}), f32[8,1,1536]{2,1,0:T(1,128)S(1)}, u32[]{:S(2)}, u32[]{:S(2)}) async-start(f32[8,1,1536]{2,1,0:T(1,128)} %reshape.598), calls=%async_computation.4 | async-start | bytes 98304 | tf_op jit(solution)/shard_map/all_to_all | solution.py:36
  12.7 2.5 copy-start.9
  12.8 2.7 copy-start.12
  15.5 2.7 copy-start.7
  33.9 11.8 %all-to-all-start.5 = ((f32[16,1,1536]{2,1,0:T(1,128)}), f32[16,1,1536]{2,1,0:T(1,128)S(1)}, u32[]{:S(2)}, u32[]{:S(2)}) async-start(f32[16,1,1536]{2,1,0:T(1,128)} %reshape.600), calls=%async_computation.5 | async-start | bytes 196608 | tf_op jit(solution)/shard_map/all_to_all | solution.py:36
  45.8 16.6 %all-to-all-start = ((bf16[8,2,8192]{2,1,0:T(2,128)(2,1)}), bf16[8,2,8192]{2,1,0:T(2,128)(2,1)S(1)}, u32[]{:S(2)}, u32[]{:S(2)}) async-start(bf16[8,2,8192]{2,1,0:T(2,128)(2,1)} %reshape.602), calls=%async_computation | async-start | bytes 524288 | tf_op jit(solution)/shard_map/all_to_all | solution.py:192
  85.9 18.5 %all-to-all-start.1 = ((bf16[8,2,64,512]{3,2,1,0:T(8,128)(2,1)}), bf16[8,2,64,512]{3,2,1,0:T(8,128)(2,1)S(1)}, u32[]{:S(2)}, u32[]{:S(2)}) async-start(bf16[8,2,64,512]{3,2,1,0:T(8,128)(2,1)} %maximum_bitcast_fusion), calls=%async_computation.1 | async-start | bytes 2097152 | tf_op jit(solution)/shard_map/all_to_all | solution.py:30
  93.6 16.4 %copy-start.4 = (f32[8,12,4096]{2,0,1:T(8,128)S(1)}, f32[8,12,4096]{2,0,1:T(8,128)}, u32[]{:S(2)}) copy-start(f32[8,12,4096]{2,0,1:T(8,128)} %param.26) | copy-start | bytes 4718596
  106.2 13.3 %all-to-all-start.2 = ((bf16[8,8,512]{2,1,0:T(8,128)(2,1)}), bf16[8,8,512]{2,1,0:T(8,128)(2,1)S(1)}, u32[]{:S(2)}, u32[]{:S(2)}) async-start(bf16[8,8,512]{2,1,0:T(8,128)(2,1)} %fusion.41), calls=%async_computation.2 | async-start | bytes 131072 | tf_op jit(solution)/shard_map/all_to_all | solution.py:227
  119.5 7.5 %copy-start.6 = (f32[4096]{0:T(1024)S(1)}, f32[4096]{0:T(1024)}, u32[]{:S(2)}) copy-start(f32[4096]{0:T(1024)} %param.23) | copy-start | bytes 49156
  119.5 51.8 %all-to-all-start.6 = ((bf16[8,3,12,4096]{3,2,1,0:T(8,128)(2,1)}), bf16[8,3,12,4096]{3,2,1,0:T(8,128)(2,1)}, u32[]{:S(2)}, u32[]{:S(2)}) async-start(bf16[8,3,12,4096]{3,2,1,0:T(8,128)(2,1)} %copy.165), calls=%async_computation.6 | async-start | bytes 6291456 | tf_op jit(solution)/shard_map/all_to_all | solution.py:175
  172.4 20.2 %all-to-all-start.3 = ((bf16[16,8,4096]{2,1,0:T(8,128)(2,1)}), bf16[16,8,4096]{2,1,0:T(8,128)(2,1)S(1)}, u32[]{:S(2)}, u32[]{:S(2)}) async-start(bf16[16,8,4096]{2,1,0:T(8,128)(2,1)} %broadcast_in_dim.215), calls=%async_computation.3 | async-start | bytes 2097152 | tf_op jit(solution)/shard_map/all_to_all | solution.py:36
  179.7 16.9 %copy-start.2 = (bf16[96,4096]{1,0:T(8,128)(2,1)}, bf16[96,4096]{1,0:T(8,128)(2,1)S(1)}, u32[]{:S(2)}) copy-start(bf16[96,4096]{1,0:T(8,128)(2,1)S(1)} %reshape_squeeze.19) | copy-start | bytes 2359300
  181.4 15.2 %copy-start.3 = (bf16[96,4096]{1,0:T(8,128)(2,1)}, bf16[96,4096]{1,0:T(8,128)(2,1)S(1)}, u32[]{:S(2)}) copy-start(bf16[96,4096]{1,0:T(8,128)(2,1)S(1)} %reshape_squeeze.18) | copy-start | bytes 2359300
  183.9 16.4 %copy-start.8 = (f32[2,64,8]{1,2,0:T(8,128)S(1)}, f32[2,64,8]{1,2,0:T(8,128)}, u32[]{:S(2)}) copy-start(f32[2,64,8]{1,2,0:T(8,128)} %param.22) | copy-start | bytes 12292
  196.6 20.2 %all-to-all-start.7 = ((bf16[16,8,4096]{2,1,0:T(8,128)(2,1)}), bf16[16,8,4096]{2,1,0:T(8,128)(2,1)S(1)}, u32[]{:S(2)}, u32[]{:S(2)}) async-start(bf16[16,8,4096]{2,1,0:T(8,128)(2,1)} %fusion.1), calls=%async_computation.7 | async-start | bytes 2097152 | tf_op jit(solution)/shard_map/all_to_all | solution.py:30
  257.3 38.5 %copy-start.1 = (bf16[8,256,512]{2,1,0:T(8,128)(2,1)S(1)}, bf16[8,256,512]{2,1,0:T(8,128)(2,1)}, u32[]{:S(2)}) copy-start(bf16[8,256,512]{2,1,0:T(8,128)(2,1)} %param.16) | copy-start | bytes 6291460
  262.8 20.2 %all-to-all-start.11 = ((bf16[16,8,4096]{2,1,0:T(8,128)(2,1)}), bf16[16,8,4096]{2,1,0:T(8,128)(2,1)S(1)}, u32[]{:S(2)}, u32[]{:S(2)}) async-start(bf16[16,8,4096]{2,1,0:T(8,128)(2,1)} %fusion.2), calls=%async_computation.11 | async-start | bytes 2097152 | tf_op jit(solution)/shard_map/all_to_all | solution.py:30
  283.9 11.0 %all-to-all-start.12 = ((bf16[8,8,512]{2,1,0:T(8,128)(2,1)}), bf16[8,8,512]{2,1,0:T(8,128)(2,1)S(1)}, u32[]{:S(2)}, u32[]{:S(2)}) async-start(bf16[8,8,512]{2,1,0:T(8,128)(2,1)} %fusion.70), calls=%async_computation.12 | async-start | bytes 131072 | tf_op jit(solution)/shard_map/all_to_all | solution.py:216

commit v2 on v0

v2 whole, which is shorter than its diff:
```python
import jax
import jax.numpy as jnp
from jax import lax
from jax.experimental import pallas as pl
from jax.experimental.pallas import tpu as pltpu
from jax.sharding import PartitionSpec as P

D = 4096
FF = 1536
QH = 64
KVH = 4
HD = 128
BLOCK = 128
WIN = 8
CAP = 8
STEPS = 2
ROWS = 64
CACHE = 256
N_FSDP = 16
N_TP = 8
SHARD = FF // (N_FSDP * N_TP)
TILES = FF // BLOCK
COLS = D // BLOCK
SHARE = D // N_TP
QUARTER = D // 4
FOLD = 4 * SHARD

neg_fill = -1e30
epsilon = 1e-06
fp_limit = 448.0
tie_nudge = 1.0 + 2.0**-22

f32 = jnp.float32
bf16 = jnp.bfloat16


def nt_dot(a, b):
    return lax.dot_general(a, b, (((1,), (1,)), ((), ())), preferred_element_type=f32)


def nn_dot(a, b):
    return lax.dot_general(a, b, (((1,), (0,)), ((), ())), preferred_element_type=f32)


def iota(shape, dim):
    return lax.broadcasted_iota(jnp.int32, shape, dim)


def kernel(
    hidden,
    queries,
    key_cache,
    value_cache,
    new_keys,
    new_values,
    lengths,
    routes,
    route_weights,
    gain,
    gate_master,
    up_master,
    down_master,
    out_proj,
    out,
    logs,
    mast,
    qbuf,
    kbuf,
    vbuf,
    wproj,
    cur,
    mine,
    x1r,
    every,
    bm,
    sendw,
    wbuf,
    sendh,
    recvh,
    sendp,
    recvp,
    slots,
    slots_t,
    share,
    mixed,
    sendd,
    recvd,
    sende,
    recve,
    sendg,
    recvg,
    sendr,
    recvr,
    spread,
    local_sem,
    x1s,
    x1q,
    x2s,
    x2q,
    hs,
    hq,
    ws,
    wq,
    cs,
    cq,
    ps,
    pq,
    ds,
    dq,
    es,
    eq,
    gs,
    gq,
    rs,
    rq,
):
    f = lax.axis_index("fsdp")
    t = lax.axis_index("tp")
    k = f // 2
    core = lax.rem(f, 2)
    partner = f + 1 - 2 * core

    def tp_peer(d):
        return lax.rem(t + d, N_TP)

    def chip_peer(d):
        return lax.rem(k + d, 8)

    def remote(src, dst, send, recv, to):
        return pltpu.make_async_remote_copy(
            src_ref=src,
            dst_ref=dst,
            send_sem=send,
            recv_sem=recv,
            device_id=to,
            device_id_type=pl.DeviceIdType.MESH,
        )

    def each(low, high, body):
        def step(d, carry):
            body(d)
            return carry

        lax.fori_loop(low, high, step, 0)

    own_cols = pl.ds(pl.multiple_of(t * SHARE, SHARE), SHARE)
    loads = [
        pltpu.make_async_copy(queries, qbuf, local_sem.at[3]),
        pltpu.make_async_copy(key_cache, kbuf, local_sem.at[4]),
        pltpu.make_async_copy(value_cache, vbuf, local_sem.at[5]),
        pltpu.make_async_copy(hidden.at[:, own_cols], cur, local_sem.at[6]),
        pltpu.make_async_copy(out_proj, wproj, local_sem.at[7]),
    ]
    for m, master in enumerate((gate_master, up_master, down_master)):

        def load_columns(c, m=m, master=master):
            cols = pl.ds(pl.multiple_of(c * BLOCK, BLOCK), BLOCK)
            pltpu.make_async_copy(master.at[:, cols], mast.at[m, c], local_sem.at[m]).start()

        each(0, COLS, load_columns)
    for load in loads:
        load.start()

    barrier = pltpu.get_barrier_semaphore()

    def greet(to):
        pl.semaphore_signal(barrier, inc=1, device_id=to, device_id_type=pl.DeviceIdType.MESH)

    each(1, N_TP, lambda d: greet((f, tp_peer(d))))
    each(1, N_FSDP, lambda d: greet((lax.rem(f + d, N_FSDP), t)))

    lane64 = iota((ROWS, ROWS), 1)
    row64 = iota((ROWS, ROWS), 0)
    earlier = (row64 < lane64).astype(f32).astype(bf16)
    expert_rows = iota((WIN, ROWS), 0)
    for s in range(STEPS):
        names = routes[s]
        weights = route_weights[s]
        total = jnp.sum(weights, axis=0, keepdims=True)
        chosen = jnp.zeros((WIN, ROWS), f32)
        shares = jnp.zeros((WIN, ROWS), f32)
        for e in range(WIN):
            match = names == e
            has = jnp.max(jnp.where(match, 1.0, 0.0), axis=0, keepdims=True)
            sums = jnp.sum(jnp.where(match, weights, 0.0), axis=0, keepdims=True)
            chosen = jnp.where(expert_rows == e, has, chosen)
            shares = jnp.where(expert_rows == e, sums, shares)
        shares = shares / total
        place = nn_dot(chosen.astype(bf16), earlier)
        place = jnp.where(chosen > 0.5, place, 1000.0)
        place_index = iota((WIN, CAP, ROWS), 1).astype(f32)
        picked = jnp.where(place[:, None, :] == place_index, 1.0, 0.0)
        picked2 = picked.reshape(WIN * CAP, ROWS)
        slots[s] = picked2.astype(bf16)
        slots_t[s] = picked2.T.astype(bf16)
        slot_share = jnp.sum(picked * shares[:, None, :], axis=2, keepdims=True)
        share[s] = jnp.broadcast_to(slot_share.reshape(WIN * CAP, 1), (WIN * CAP, BLOCK))
    column = iota((8 * FOLD, 8 * FOLD), 1)
    line = iota((8 * FOLD, 8 * FOLD), 0)
    same = ((column // FOLD) == (line // FOLD)) & (lax.rem(column, SHARD) == lax.rem(line, SHARD))
    spread[...] = jnp.where(same, 1.0, 0.0).astype(bf16)

    first_tile = (f * (N_TP * SHARD)) // BLOCK
    first_row = (f * N_TP + t) * SHARD
    border = (first_tile + 1) * BLOCK - first_row
    lane = iota((WIN, BLOCK), 1)
    zero = jnp.zeros((WIN, BLOCK), f32)
    near_max, far_max = zero, zero
    for m in range(3):
        pltpu.make_async_copy(mast.at[m], mast.at[m], local_sem.at[m]).wait()

        def tile_max(c, carry, m=m):
            near_acc, far_acc = carry
            near = zero
            far = zero
            for i in range(SHARD):
                x = jnp.abs(mast[m, c, i * WIN : (i + 1) * WIN, :])
                inside = jnp.where(i < border, 1.0, 0.0)
                near = jnp.maximum(near, x * inside)
                far = jnp.maximum(far, x * (1.0 - inside))
            here = lane == m * COLS + c
            near_acc = jnp.where(here, jnp.max(near, axis=1, keepdims=True), near_acc)
            far_acc = jnp.where(here, jnp.max(far, axis=1, keepdims=True), far_acc)
            return near_acc, far_acc

        near_max, far_max = lax.fori_loop(0, COLS, tile_max, (near_max, far_max), unroll=4)
    mine[:, :BLOCK] = near_max
    mine[:, BLOCK:] = far_max

    pl.semaphore_wait(barrier, N_TP - 1 + N_FSDP - 1)

    def x1(d):
        return remote(mine, x1r.at[d], x1s.at[d], x1q.at[d], (f, tp_peer(d)))

    each(1, N_TP, lambda d: x1(d).start())

    for load in loads[:3]:
        load.wait()
    row_of = lax.rem(iota((16, HD), 0), 8)
    keep_tile = [jnp.where(row_of == r, 1.0, 0.0).astype(bf16) for r in range(8)]
    keep = [jnp.concatenate([m] * 16, axis=0) for m in keep_tile]
    keep_wide = [jnp.concatenate([m, m], axis=1) for m in keep]
    sub = iota((8, CACHE), 0)
    live = jnp.zeros((8, CACHE), jnp.int32)
    for r in range(8):
        live = jnp.where(sub == r, lengths[r], live)
    alive = (iota((8, CACHE), 1) < live)[None]
    lead = lax.rem(iota((32, 8, 16), 0), 2)
    fresh_col = iota((32, 8, 16), 2)
    fresh_ok = (lax.rem(fresh_col, 8) == iota((32, 8, 16), 1)) & (fresh_col // 8 <= lead)

    def attend(g):
        wide = pl.ds(pl.multiple_of(g * 2048, 2048), 2048)
        cols = pl.ds(pl.multiple_of(g * HD, HD), HD)
        flat = qbuf[:, wide]
        q = jnp.concatenate([flat[:, h * HD : (h + 1) * HD] for h in range(16)], axis=0)
        q_wide = jnp.concatenate([q * keep[r] for r in range(8)], axis=1)
        k_wide = jnp.concatenate([kbuf[r, :, cols] for r in range(8)], axis=1)
        scores = (nt_dot(q_wide, k_wide) * HD**-0.5).reshape(32, 8, CACHE)
        fresh = (nt_dot(q, new_keys[:, cols]) * HD**-0.5).reshape(32, 8, 16)
        peak = jnp.maximum(
            jnp.max(jnp.where(alive, scores, neg_fill), axis=2, keepdims=True),
            jnp.max(jnp.where(fresh_ok, fresh, neg_fill), axis=2, keepdims=True),
        )
        weights = jnp.where(alive, jnp.exp(scores - peak), 0.0)
        fresh_weights = jnp.where(fresh_ok, jnp.exp(jnp.minimum(fresh - peak, 0.0)), 0.0)
        total = jnp.sum(weights, axis=2, keepdims=True) + jnp.sum(
            fresh_weights, axis=2, keepdims=True
        )
        inverse = 1.0 / total
        probs = (weights * inverse).reshape(256, CACHE).astype(bf16)
        fresh_probs = (fresh_weights * inverse).reshape(256, 16).astype(bf16)
        p_wide = jnp.concatenate([probs * keep_wide[r] for r in range(8)], axis=1)
        v_tall = jnp.concatenate([vbuf[r, :, cols] for r in range(8)], axis=0)
        heads = nn_dot(p_wide, v_tall) + nn_dot(fresh_probs, new_values[:, cols])
        heads = heads.astype(bf16)
        for half in range(2):
            parts = [heads[(half * 8 + h) * 16 : (half * 8 + h + 1) * 16] for h in range(8)]
            sendh[2 * g + half] = jnp.concatenate(parts, axis=1)

    each(0, 2, attend)

    each(1, N_TP, lambda d: x1(d).wait_recv())
    group = mine[...]
    for d in range(1, N_TP):
        group = jnp.maximum(group, x1r[d])
    every[f] = group

    def x2(d):
        return remote(
            every.at[f], every.at[f], x2s.at[d], x2q.at[d], (lax.rem(f + d, N_FSDP), t)
        )

    each(1, N_FSDP, lambda d: x2(d).start())

    each(2, KVH, attend)

    def send_heads(d):
        return remote(
            sendh.at[tp_peer(d)], recvh.at[t], hs.at[d], hq.at[d], (f, tp_peer(d))
        )

    each(1, N_TP, lambda d: send_heads(d).start())
    recvh[t] = sendh[t]

    each(1, N_FSDP, lambda d: x2(d).wait_recv())
    for tile in range(TILES):
        parts = []
        for owner in range(N_FSDP):
            first = owner * N_TP * SHARD // BLOCK
            last = (owner * N_TP * SHARD + N_TP * SHARD - 1) // BLOCK
            if first == tile:
                parts.append(every[owner, :, :BLOCK])
            if last == tile and last != first:
                parts.append(every[owner, :, BLOCK:])
        tile_maxima = parts[0]
        for part in parts[1:]:
            tile_maxima = jnp.maximum(tile_maxima, part)
        bm[tile] = tile_maxima
        log = jnp.log2((tile_maxima + epsilon) / fp_limit)
        for m in range(3):
            logs[m, tile] = log[:, m * COLS : (m + 1) * COLS]

    scales = [
        (bm[first_tile] + epsilon) / fp_limit,
        (bm[jnp.minimum(first_tile + 1, TILES - 1)] + epsilon) / fp_limit,
    ]
    inverses = [tie_nudge / scale for scale in scales]

    for m in range(3):

        def restore(c, carry, m=m):
            here = lane == m * COLS + c
            near_scale, far_scale, near_inv, far_inv = (
                jnp.sum(jnp.where(here, table, 0.0), axis=1, keepdims=True)
                for table in scales + inverses
            )
            for i in range(SHARD):
                rows = slice(i * WIN, (i + 1) * WIN)
                value = mast[m, c, rows, :] * jnp.where(i < border, near_inv, far_inv)
                grid = value.astype(jnp.float8_e4m3fn).astype(f32)
                mast[m, c, rows, :] = grid * jnp.where(i < border, near_scale, far_scale)
            return carry

        lax.fori_loop(0, COLS, restore, 0, unroll=2)

    def quantize(e, d):
        for m in range(3):

            def piece(c, carry, m=m):
                parts = [
                    mast[m, quarter * (QUARTER // BLOCK) + c, pl.ds(e, SHARD, stride=WIN), :]
                    for quarter in range(4)
                ]
                cols = pl.ds(pl.multiple_of(c * BLOCK, BLOCK), BLOCK)
                sendw[d, m, :, cols] = jnp.concatenate(parts, axis=0).astype(bf16)
                return carry

            lax.fori_loop(0, QUARTER // BLOCK, piece, 0, unroll=4)

    def send_weights(d):
        return remote(
            sendw.at[d], wbuf.at[0, :, t], ws.at[d], wq.at[d], (f, tp_peer(d))
        )

    def convert(d):
        quantize(tp_peer(d), d)
        send_weights(d).start()

    each(1, N_TP, convert)

    def pass_on(d):
        origin = lax.rem(t + N_TP - d, N_TP)
        return remote(
            wbuf.at[0, :, origin], wbuf.at[1, :, origin], cs.at[d], cq.at[d], (partner, t)
        )

    quantize(t, 0)
    for m in range(3):
        wbuf[0, m, t] = sendw[0, m]
    pass_on(0).start()

    loads[4].wait()
    each(1, N_TP, lambda d: send_heads(d).wait_recv())

    def send_projected(s, d):
        return remote(
            sendp.at[s, d], recvp.at[s, t], ps.at[s, d], pq.at[s, d], (f, tp_peer(d))
        )

    def project(i):
        d = lax.rem(i, N_TP)
        cols = pl.ds(pl.multiple_of(tp_peer(d) * SHARE, SHARE), SHARE)
        rows = recvh[...].reshape(STEPS * ROWS, QH * HD // N_TP)
        result = nn_dot(rows, wproj[:, cols]).reshape(8, STEPS, 8, SHARE)
        for s in range(STEPS):
            sendp[s, d] = result[:, s].reshape(ROWS, SHARE).astype(bf16)

        @pl.when(d != 0)
        def _():
            for s in range(STEPS):
                send_projected(s, d).start()

    each(1, N_TP + 1, project)
    for s in range(STEPS):
        recvp[s, t] = sendp[s, 0]
    loads[3].wait()

    quarter_of = lax.rem(iota((WIN * CAP, 8 * FOLD), 1), FOLD) // SHARD
    own_share = pl.ds(pl.multiple_of(t * CAP, CAP), CAP)

    def send_slots(s, d):
        return remote(
            sendd.at[s, tp_peer(d)], recvd.at[s, t], ds.at[s, d], dq.at[s, d], (f, tp_peer(d))
        )

    def send_normed(s, d):
        to = 2 * chip_peer(d) + core
        return remote(sende.at[s], recve.at[s, k], es.at[s, d], eq.at[s, d], (to, t))

    def send_partial(s, d):
        to = 2 * chip_peer(d) + core
        return remote(
            sendg.at[s, chip_peer(d)], recvg.at[s, k], gs.at[s, d], gq.at[s, d], (to, t)
        )

    def send_back(s, d):
        return remote(
            sendr.at[s, tp_peer(d)], recvr.at[s, t], rs.at[s, d], rq.at[s, d], (f, tp_peer(d))
        )

    def gathered(s, half, m):
        rows = recve[s].reshape(128, 2048)
        rows = jnp.concatenate([rows[:, :QUARTER], rows[:, QUARTER:]], axis=0)
        product = nt_dot(rows, wbuf[half, m].reshape(8 * FOLD, QUARTER))
        product = product.reshape(2, 8, 2, CAP, 8 * FOLD)
        by = [product[q % 2, :, q // 2].reshape(WIN * CAP, 8 * FOLD) for q in range(4)]
        parts = jnp.where(
            quarter_of == 0,
            by[0],
            jnp.where(quarter_of == 1, by[1], jnp.where(quarter_of == 2, by[2], by[3])),
        )
        high = parts.astype(bf16)
        rest = parts - high.astype(f32)
        middle = rest.astype(bf16)
        low = (rest - middle.astype(f32)).astype(bf16)
        split = nn_dot(jnp.concatenate([high, middle, low], axis=0), spread[...])
        split = split.reshape(3, WIN * CAP, 8 * FOLD)
        return split[0] + split[1] + split[2]

    def decode(s):
        each(1, N_TP, lambda d: send_projected(s, d).wait_recv())
        projected = recvp[s, 0].astype(f32)
        for j in range(1, N_TP):
            projected = projected + recvp[s, j].astype(f32)
        mix = (cur[...].astype(f32) + projected).astype(bf16)
        mixed[s] = mix
        sendd[s] = nn_dot(slots[s], mix).reshape(WIN, CAP, SHARE)
        each(1, N_TP, lambda d: send_slots(s, d).start())
        recvd[s, t] = sendd[s, t]
        each(1, N_TP, lambda d: send_slots(s, d).wait_recv())
        blocks = [recvd[s, j] for j in range(N_TP)]
        squares = blocks[0] * blocks[0]
        for block in blocks[1:]:
            squares = squares + block * block
        squares = jnp.sum(squares, axis=1, keepdims=True)
        inverse = lax.rsqrt(squares * (1.0 / D) + epsilon)
        normed = [
            blocks[j] * inverse * gain[:, j * SHARE : (j + 1) * SHARE] for j in range(N_TP)
        ]
        folded = jnp.concatenate(
            [jnp.concatenate(normed[:4], axis=1), jnp.concatenate(normed[4:], axis=1)], axis=0
        ).astype(bf16)
        sende[s] = folded
        each(1, 8, lambda d: send_normed(s, d).start())
        recve[s, k] = folded

        @pl.when(s == 0)
        def _():
            def forward(d):
                send_weights(d).wait_recv()
                pass_on(d).start()

            each(1, N_TP, forward)
            each(0, N_TP, lambda d: pass_on(d).wait_recv())

        each(1, 8, lambda d: send_normed(s, d).wait_recv())
        total = jnp.zeros((4 * WIN * CAP, QUARTER), f32)
        for half in range(2):
            gate = gathered(s, half, 0)
            up = gathered(s, half, 1)
            act = gate / (1.0 + jnp.exp(-gate)) * up
            stacked = jnp.concatenate(
                [jnp.where(quarter_of == q, act, 0.0) for q in range(4)], axis=0
            ).astype(bf16)
            total = total + nn_dot(stacked, wbuf[half, 2].reshape(8 * FOLD, QUARTER))
        total = total.reshape(4, 8, CAP, QUARTER)
        halves = [jnp.concatenate([total[2 * h], total[2 * h + 1]], axis=2) for h in range(2)]
        sendg[s] = jnp.concatenate(halves, axis=1).astype(bf16)
        each(1, 8, lambda d: send_partial(s, d).start())
        recvg[s, k] = sendg[s, k]
        each(1, 8, lambda d: send_partial(s, d).wait_recv())
        summed = recvg[s, 0].astype(f32)
        for j in range(1, 8):
            summed = summed + recvg[s, j].astype(f32)
        summed = summed.reshape(2, CAP, 2048) * share[s, own_share, :1][None]
        for j in range(N_TP):
            sendr[s, j] = summed[j // 4, :, (j % 4) * SHARE : (j % 4 + 1) * SHARE]
        each(1, N_TP, lambda d: send_back(s, d).start())
        recvr[s, t] = sendr[s, t]
        each(1, N_TP, lambda d: send_back(s, d).wait_recv())
        returned = recvr[s].reshape(WIN * CAP, SHARE).astype(bf16)
        moe = nn_dot(slots_t[s], returned)
        cur[...] = (mixed[s].astype(f32) + moe).astype(bf16)

    each(0, STEPS, decode)
    out[...] = cur[...]

    each(1, N_FSDP, lambda d: x2(d).wait_send())
    each(0, N_TP, lambda d: pass_on(d).wait_send())

    def drain(d):
        x1(d).wait_send()
        send_heads(d).wait_send()
        send_weights(d).wait_send()
        for s in range(STEPS):
            send_projected(s, d).wait_send()
            send_slots(s, d).wait_send()
            send_normed(s, d).wait_send()
            send_partial(s, d).wait_send()
            send_back(s, d).wait_send()

    each(1, N_TP, drain)


def local(
    hidden_in,
    queries,
    key_cache,
    value_cache,
    new_keys,
    new_values,
    lengths,
    routes,
    route_weights,
    norm_gain,
    gate_master,
    up_master,
    down_master,
    out_proj,
):
    def flat(master):
        return master.transpose(1, 0, 2).reshape(SHARD * WIN, D)

    vmem = pl.BlockSpec(memory_space=pltpu.VMEM)
    smem = pl.BlockSpec(memory_space=pltpu.SMEM)
    far = pl.BlockSpec(memory_space=pl.ANY)
    dma = pltpu.SemaphoreType.DMA
    v = pltpu.VMEM
    scratch = [
        v((3, COLS, SHARD * WIN, BLOCK), f32),
        v((16, QH * HD), bf16),
        v((8, CACHE, KVH * HD), bf16),
        v((8, CACHE, KVH * HD), bf16),
        v((QH * HD // N_TP, D), bf16),
        v((ROWS, SHARE), bf16),
        v((WIN, 2 * BLOCK), f32),
        v((N_TP, WIN, 2 * BLOCK), f32),
        v((N_FSDP, WIN, 2 * BLOCK), f32),
        v((TILES, WIN, BLOCK), f32),
        v((N_TP, 3, FOLD, QUARTER), bf16),
        v((2, 3, N_TP, FOLD, QUARTER), bf16),
        v((N_TP, 16, 1024), bf16),
        v((N_TP, 16, 1024), bf16),
        v((STEPS, N_TP, ROWS, SHARE), bf16),
        v((STEPS, N_TP, ROWS, SHARE), bf16),
        v((STEPS, WIN * CAP, ROWS), bf16),
        v((STEPS, ROWS, WIN * CAP), bf16),
        v((STEPS, WIN * CAP, BLOCK), f32),
        v((STEPS, ROWS, SHARE), bf16),
        v((STEPS, WIN, CAP, SHARE), f32),
        v((STEPS, N_TP, CAP, SHARE), f32),
        v((STEPS, 16, 2048), bf16),
        v((STEPS, 8, 16, 2048), bf16),
        v((STEPS, 8, 16, 2048), bf16),
        v((STEPS, 8, 16, 2048), bf16),
        v((STEPS, N_TP, CAP, SHARE), f32),
        v((STEPS, N_TP, CAP, SHARE), f32),
        v((8 * FOLD, 8 * FOLD), bf16),
        dma((8,)),
        dma((N_TP,)),
        dma((N_TP,)),
        dma((N_FSDP,)),
        dma((N_FSDP,)),
    ]
    scratch += [dma((N_TP,)) for _ in range(6)]
    scratch += [dma((STEPS, N_TP)) for _ in range(10)]
    out, logs = pl.pallas_call(
        kernel,
        out_shape=(
            jax.ShapeDtypeStruct((ROWS, SHARE), bf16),
            jax.ShapeDtypeStruct((3, TILES, WIN, COLS), f32),
        ),
        in_specs=[far, far, far, far, vmem, vmem, smem, vmem, vmem, vmem, far, far, far, far],
        out_specs=(vmem, vmem),
        scratch_shapes=scratch,
        compiler_params=pltpu.CompilerParams(
            collective_id=0, has_side_effects=True, vmem_limit_bytes=58 << 20
        ),
    )(
        hidden_in,
        queries.reshape(16, QH * HD),
        key_cache,
        value_cache,
        new_keys.reshape(16, KVH * HD),
        new_values.reshape(16, KVH * HD),
        lengths,
        routes.transpose(0, 2, 1),
        route_weights.transpose(0, 2, 1),
        norm_gain.reshape(1, D),
        flat(gate_master),
        flat(up_master),
        flat(down_master),
        out_proj,
    )
    return (out, logs.transpose(0, 2, 1, 3))


def solution(mesh):
    in_specs = (
        P("fsdp", None),
        P(None, ("fsdp", "tp"), None),
        P(("fsdp", "tp"), None, None),
        P(("fsdp", "tp"), None, None),
        P(None, ("fsdp", "tp"), None),
        P(None, ("fsdp", "tp"), None),
        P(("fsdp", "tp")),
        P(None, "fsdp", None),
        P(None, "fsdp", None),
        P(),
        P(None, ("fsdp", "tp"), None),
        P(None, ("fsdp", "tp"), None),
        P(None, ("fsdp", "tp"), None),
        P("tp", None),
    )
    out_specs = (P("fsdp", "tp"), P())
    return jax.shard_map(local, mesh=mesh, in_specs=in_specs, out_specs=out_specs, check_vma=False)
```

time: 579 us -> 136 us (0.23)
  waiting for transfers between devices: 167 us -> 0 us
  Pallas kernels: 0 us -> 132 us
  blocking collectives: 115 us -> 0 us
  local copies, waits for them, and re-layouts: 95.3 us -> 3.05 us
  other arithmetic: 90.6 us -> 0 us
  matrix products: 61.6 us -> 0 us
  starting transfers between devices: 31.9 us -> 0 us
  between operations: 14.5 us -> 0.64 us
    pallas_call x0 -> x1, Pallas kernels: none -> 132 us  [local(): pl.pallas_call(kernel, out_shape=(jax.ShapeDtypeStruct((ROWS, SHARE), bf1...]
    all_gather x1 -> x0, waiting for transfers between devices: 122 us -> none  [local(): gathered = lax.all_gather(quantized, 'fsdp', axis=2, tiled=True)]
    pmax x1 -> x0, blocking collectives: 69.4 us -> none  [local(): block_max = lax.pmax(partial_max, ('fsdp', 'tp'))]
    dot_general x19 -> x0, matrix products: 61.6 us -> none  [the longest x2 25.1 us: expert_rows(): jnp.einsum('ech,ehd->ecd', product, down_rows, preferred_element_type=jnp...]
    squeeze x3 -> x0, local copies, waits for them, and re-layouts: 57.9 us -> none  [local_experts(): outputs = expert_rows(selected, restored[0], restored[1], restored[2])]
    convert_element_type x7 -> x0, other arithmetic: 47.3 us -> none  [the longest x1 38.8 us: dequantize(): (tiles * factors[..., None]).astype(jnp.bfloat16).reshape(3, WIN, count, D)]
    psum x2 -> x0, blocking collectives: 46.1 us -> none  [local(): squares = lax.psum(jnp.sum(values * values, axis=1), 'tp')]
    all_to_all x8 -> x0, waiting for transfers between devices: 44.7 us -> none  [the longest x4 27.3 us: sent_and_summed(): lax.all_to_all(blocks, axis, split_axis=0, concat_axis=0, tiled=True)]
  transfers between devices with their start and end apart: 9 -> 0, of which waited for: 7 -> 0; matrix products, arithmetic and copies ran while one was open for 36% -> 0% of each run, Pallas kernels for 0% -> 0%
where the time goes in v2:
time: 136 us
  Pallas kernels  132 us (97%)
  local copies, waits for them, and re-layouts  3.05 us (2%)
    pallas_call x1, Pallas kernels, local(): pl.pallas_call(kernel, out_shape=(jax.ShapeDtypeStruct((ROWS, SHARE), bf1...  132 us
    unnamed x2, local copies, waits for them, and re-layouts  3.05 us

profile of v2, /device:TPU:0, one launch (start us, length us, event | category | flops | bytes accessed | tf_op | source)
XLA Modules:
  0.0 136.2 jit_solution(13067749803475709635)
XLA Ops:
  0.6 132.5 %shard_map.149 = (bf16[64,512]{1,0:T(8,128)(2,1)}, f32[3,12,8,32]{3,2,1,0:T(8,128)}) custom-call(bf16[64,4096]{1,0:T(8,128)(2,1)} %hidden.1, bf16[16,8192]{1,0:T(8,128)(2,1)} %bitcast.19, bf16[8,256,512]{2,1,0:T(8,128)(2,1)} %key_cache.1, bf16[8,256,512]{2,1,0:T(8,128)(2,1)} %value_cache.1, bf16[16,512]{1,0:T(8,128)(2,1)} %bitcast.21, ...), custom_call_target="tpu_custom_call" | custom-call | tf_op jit(solution)/shard_map/pallas_call | solution.py:598
  133.1 1.5 %copy.18 = bf16[64,512]{1,0:T(8,128)(2,1)} copy(bf16[64,512]{1,0:T(8,128)(2,1)} %get-tuple-element.8) | data formatting | bytes 131072
  134.6 1.6 %copy.19 = f32[3,8,12,32]{3,1,2,0:T(8,128)} copy(f32[3,8,12,32]{3,1,2,0:T(8,128)} %bitcast.20) | data formatting | bytes 73728

commit v3 on v2

--- a/solution.py
+++ b/solution.py
@@ -22,6 +22,7 @@
 TILES = FF // BLOCK
 COLS = D // BLOCK
 SHARE = D // N_TP
+NEAR = 4 * N_TP
 QUARTER = D // 4
 FOLD = 4 * SHARD
 
@@ -72,7 +73,6 @@
     mine,
     x1r,
     every,
-    bm,
     sendw,
     wbuf,
     sendh,
@@ -143,6 +143,20 @@
 
         lax.fori_loop(low, high, step, 0)
 
+    barrier = pltpu.get_barrier_semaphore()
+
+    def greet(to):
+        pl.semaphore_signal(barrier, inc=1, device_id=to, device_id_type=pl.DeviceIdType.MESH)
+
+    def near_peer(d):
+        return (f // 4) * 4 + lax.rem(lax.rem(f, 4) + d // N_TP, 4), lax.rem(t + d, N_TP)
+
+    def far_peer(d):
+        return 4 * lax.rem(f // 4 + 1 + d // 2, 4) + 2 * lax.rem(d, 2) + core, t
+
+    each(1, NEAR, lambda d: greet(near_peer(d)))
+    each(0, 6, lambda d: greet(far_peer(d)))
+
     own_cols = pl.ds(pl.multiple_of(t * SHARE, SHARE), SHARE)
     loads = [
         pltpu.make_async_copy(queries, qbuf, local_sem.at[3]),
@@ -153,21 +167,13 @@
     ]
     for m, master in enumerate((gate_master, up_master, down_master)):
 
-        def load_columns(c, m=m, master=master):
-            cols = pl.ds(pl.multiple_of(c * BLOCK, BLOCK), BLOCK)
-            pltpu.make_async_copy(master.at[:, cols], mast.at[m, c], local_sem.at[m]).start()
-
-        each(0, COLS, load_columns)
+        def load_rows(i, m=m, master=master):
+            rows = pl.ds(pl.multiple_of(i * WIN, WIN), WIN)
+            pltpu.make_async_copy(master.at[i], mast.at[m, :, rows], local_sem.at[m]).start()
+
+        each(0, SHARD, load_rows)
     for load in loads:
         load.start()
-
-    barrier = pltpu.get_barrier_semaphore()
-
-    def greet(to):
-        pl.semaphore_signal(barrier, inc=1, device_id=to, device_id_type=pl.DeviceIdType.MESH)
-
-    each(1, N_TP, lambda d: greet((f, tp_peer(d))))
-    each(1, N_FSDP, lambda d: greet((lax.rem(f + d, N_FSDP), t)))
 
     lane64 = iota((ROWS, ROWS), 1)
     row64 = iota((ROWS, ROWS), 0)
@@ -227,12 +233,15 @@
     mine[:, :BLOCK] = near_max
     mine[:, BLOCK:] = far_max
 
-    pl.semaphore_wait(barrier, N_TP - 1 + N_FSDP - 1)
+    pl.semaphore_wait(barrier, NEAR - 1 + 6)
+
+    place_here = lax.rem(f, 4) * N_TP + t
 
     def x1(d):
-        return remote(mine, x1r.at[d], x1s.at[d], x1q.at[d], (f, tp_peer(d)))
-
-    each(1, N_TP, lambda d: x1(d).start())
+        return remote(mine, x1r.at[place_here], x1s.at[d], x1q.at[d], near_peer(d))
+
+    each(1, NEAR, lambda d: x1(d).start())
+    x1r[place_here] = mine[...]
 
     for load in loads[:3]:
         load.wait()
@@ -278,22 +287,7 @@
             parts = [heads[(half * 8 + h) * 16 : (half * 8 + h + 1) * 16] for h in range(8)]
             sendh[2 * g + half] = jnp.concatenate(parts, axis=1)
 
-    each(0, 2, attend)
-
-    each(1, N_TP, lambda d: x1(d).wait_recv())
-    group = mine[...]
-    for d in range(1, N_TP):
-        group = jnp.maximum(group, x1r[d])
-    every[f] = group
-
-    def x2(d):
-        return remote(
-            every.at[f], every.at[f], x2s.at[d], x2q.at[d], (lax.rem(f + d, N_FSDP), t)
-        )
-
-    each(1, N_FSDP, lambda d: x2(d).start())
-
-    each(2, KVH, attend)
+    each(0, KVH, attend)
 
     def send_heads(d):
         return remote(
@@ -303,33 +297,38 @@
     each(1, N_TP, lambda d: send_heads(d).start())
     recvh[t] = sendh[t]
 
-    each(1, N_FSDP, lambda d: x2(d).wait_recv())
-    for tile in range(TILES):
-        parts = []
-        for owner in range(N_FSDP):
-            first = owner * N_TP * SHARD // BLOCK
-            last = (owner * N_TP * SHARD + N_TP * SHARD - 1) // BLOCK
-            if first == tile:
-                parts.append(every[owner, :, :BLOCK])
-            if last == tile and last != first:
-                parts.append(every[owner, :, BLOCK:])
-        tile_maxima = parts[0]
-        for part in parts[1:]:
-            tile_maxima = jnp.maximum(tile_maxima, part)
-        bm[tile] = tile_maxima
-        log = jnp.log2((tile_maxima + epsilon) / fp_limit)
-        for m in range(3):
-            logs[m, tile] = log[:, m * COLS : (m + 1) * COLS]
-
+    each(1, NEAR, lambda d: x1(d).wait_recv())
+    quad = f // 4
+    for tile in range(3):
+        first = x1r[tile * N_TP, :, BLOCK if tile else 0 : 2 * BLOCK if tile else BLOCK]
+        for j in range(N_TP):
+            if tile:
+                first = jnp.maximum(first, x1r[tile * N_TP + j, :, BLOCK:])
+            else:
+                first = jnp.maximum(first, x1r[j, :, :BLOCK])
+            first = jnp.maximum(first, x1r[(tile + 1) * N_TP + j, :, :BLOCK])
+        every[quad, tile] = first
+
+    def x2(d):
+        to = 4 * lax.rem(quad + d, 4) + lax.rem(f, 4)
+        return remote(every.at[quad], every.at[quad], x2s.at[d], x2q.at[d], (to, t))
+
+    each(1, 4, lambda d: x2(d).start())
+
+    near_tile = first_tile - 3 * quad
     scales = [
-        (bm[first_tile] + epsilon) / fp_limit,
-        (bm[jnp.minimum(first_tile + 1, TILES - 1)] + epsilon) / fp_limit,
+        (every[quad, near_tile] + epsilon) / fp_limit,
+        (every[quad, jnp.minimum(near_tile + 1, 2)] + epsilon) / fp_limit,
     ]
     inverses = [tie_nudge / scale for scale in scales]
 
-    for m in range(3):
-
-        def restore(c, carry, m=m):
+    def send_weights(m, d):
+        return remote(
+            sendw.at[m, d], wbuf.at[0, m, t], ws.at[m, d], wq.at[m, d], (f, tp_peer(d))
+        )
+
+    def convert_matrix(m):
+        def restore(c, carry):
             here = lane == m * COLS + c
             near_scale, far_scale, near_inv, far_inv = (
                 jnp.sum(jnp.where(here, table, 0.0), axis=1, keepdims=True)
@@ -344,41 +343,29 @@
 
         lax.fori_loop(0, COLS, restore, 0, unroll=2)
 
-    def quantize(e, d):
-        for m in range(3):
-
-            def piece(c, carry, m=m):
+        def convert(i):
+            d = lax.rem(i, N_TP)
+            e = tp_peer(d)
+
+            def piece(c, carry):
                 parts = [
                     mast[m, quarter * (QUARTER // BLOCK) + c, pl.ds(e, SHARD, stride=WIN), :]
                     for quarter in range(4)
                 ]
                 cols = pl.ds(pl.multiple_of(c * BLOCK, BLOCK), BLOCK)
-                sendw[d, m, :, cols] = jnp.concatenate(parts, axis=0).astype(bf16)
+                sendw[m, d, :, cols] = jnp.concatenate(parts, axis=0).astype(bf16)
                 return carry
 
             lax.fori_loop(0, QUARTER // BLOCK, piece, 0, unroll=4)
 
-    def send_weights(d):
-        return remote(
-            sendw.at[d], wbuf.at[0, :, t], ws.at[d], wq.at[d], (f, tp_peer(d))
-        )
-
-    def convert(d):
-        quantize(tp_peer(d), d)
-        send_weights(d).start()
-
-    each(1, N_TP, convert)
-
-    def pass_on(d):
-        origin = lax.rem(t + N_TP - d, N_TP)
-        return remote(
-            wbuf.at[0, :, origin], wbuf.at[1, :, origin], cs.at[d], cq.at[d], (partner, t)
-        )
-
-    quantize(t, 0)
-    for m in range(3):
-        wbuf[0, m, t] = sendw[0, m]
-    pass_on(0).start()
+            @pl.when(d != 0)
+            def _():
+                send_weights(m, d).start()
+
+        each(1, N_TP + 1, convert)
+        wbuf[0, m, t] = sendw[m, 0]
+
+    convert_matrix(0)
 
     loads[4].wait()
     each(1, N_TP, lambda d: send_heads(d).wait_recv())
@@ -398,13 +385,23 @@
 
         @pl.when(d != 0)
         def _():
-            for s in range(STEPS):
-                send_projected(s, d).start()
+            send_projected(0, d).start()
 
     each(1, N_TP + 1, project)
     for s in range(STEPS):
         recvp[s, t] = sendp[s, 0]
     loads[3].wait()
+
+    convert_matrix(1)
+    convert_matrix(2)
+
+    def pass_on(d):
+        origin = lax.rem(t + N_TP - d, N_TP)
+        return remote(
+            wbuf.at[0, :, origin], wbuf.at[1, :, origin], cs.at[d], cq.at[d], (partner, t)
+        )
+
+    pass_on(0).start()
 
     quarter_of = lax.rem(iota((WIN * CAP, 8 * FOLD), 1), FOLD) // SHARD
     own_share = pl.ds(pl.multiple_of(t * CAP, CAP), CAP)
@@ -478,10 +475,12 @@
         @pl.when(s == 0)
         def _():
             def forward(d):
-                send_weights(d).wait_recv()
+                for m in range(3):
+                    send_weights(m, d).wait_recv()
                 pass_on(d).start()
 
             each(1, N_TP, forward)
+            each(1, N_TP, lambda d: send_projected(1, d).start())
             each(0, N_TP, lambda d: pass_on(d).wait_recv())
 
         each(1, 8, lambda d: send_normed(s, d).wait_recv())
@@ -516,13 +515,19 @@
     each(0, STEPS, decode)
     out[...] = cur[...]
 
-    each(1, N_FSDP, lambda d: x2(d).wait_send())
+    each(1, 4, lambda d: x2(d).wait_recv())
+    for tile in range(TILES):
+        log = jnp.log2((every[tile // 3, tile % 3] + epsilon) / fp_limit)
+        for m in range(3):
+            logs[m, tile] = log[:, m * COLS : (m + 1) * COLS]
+    each(1, 4, lambda d: x2(d).wait_send())
+    each(1, NEAR, lambda d: x1(d).wait_send())
     each(0, N_TP, lambda d: pass_on(d).wait_send())
 
     def drain(d):
-        x1(d).wait_send()
         send_heads(d).wait_send()
-        send_weights(d).wait_send()
+        for m in range(3):
+            send_weights(m, d).wait_send()
         for s in range(STEPS):
             send_projected(s, d).wait_send()
             send_slots(s, d).wait_send()
@@ -550,7 +555,8 @@
     out_proj,
 ):
     def flat(master):
-        return master.transpose(1, 0, 2).reshape(SHARD * WIN, D)
+        blocks = master.transpose(1, 0, 2).reshape(SHARD, WIN, COLS, BLOCK)
+        return blocks.transpose(0, 2, 1, 3)
 
     vmem = pl.BlockSpec(memory_space=pltpu.VMEM)
     smem = pl.BlockSpec(memory_space=pltpu.SMEM)
@@ -565,10 +571,9 @@
         v((QH * HD // N_TP, D), bf16),
         v((ROWS, SHARE), bf16),
         v((WIN, 2 * BLOCK), f32),
-        v((N_TP, WIN, 2 * BLOCK), f32),
-        v((N_FSDP, WIN, 2 * BLOCK), f32),
-        v((TILES, WIN, BLOCK), f32),
-        v((N_TP, 3, FOLD, QUARTER), bf16),
+        v((NEAR, WIN, 2 * BLOCK), f32),
+        v((4, 3, WIN, BLOCK), f32),
+        v((3, N_TP, FOLD, QUARTER), bf16),
         v((2, 3, N_TP, FOLD, QUARTER), bf16),
         v((N_TP, 16, 1024), bf16),
         v((N_TP, 16, 1024), bf16),
@@ -588,12 +593,17 @@
         v((STEPS, N_TP, CAP, SHARE), f32),
         v((8 * FOLD, 8 * FOLD), bf16),
         dma((8,)),
+        dma((NEAR,)),
+        dma((NEAR,)),
+        dma((4,)),
+        dma((4,)),
         dma((N_TP,)),
         dma((N_TP,)),
-        dma((N_FSDP,)),
-        dma((N_FSDP,)),
+        dma((3, N_TP)),
+        dma((3, N_TP)),
+        dma((N_TP,)),
+        dma((N_TP,)),
     ]
-    scratch += [dma((N_TP,)) for _ in range(6)]
     scratch += [dma((STEPS, N_TP)) for _ in range(10)]
     out, logs = pl.pallas_call(
         kernel,

time: 136 us -> 120 us (0.88)
  Pallas kernels: 132 us -> 116 us
    pallas_call x1, Pallas kernels: 132 us -> 116 us  [local(): pl.pallas_call(kernel, out_shape=(jax.ShapeDtypeStruct((ROWS, SHARE), bf1...]
where the time goes in v3:
time: 120 us
  Pallas kernels  116 us (97%)
  local copies, waits for them, and re-layouts  3.05 us (3%)
    pallas_call x1, Pallas kernels, local(): pl.pallas_call(kernel, out_shape=(jax.ShapeDtypeStruct((ROWS, SHARE), bf1...  116 us
    unnamed x2, local copies, waits for them, and re-layouts  3.05 us

profile of v3, /device:TPU:0, one launch (start us, length us, event | category | flops | bytes accessed | tf_op | source)
XLA Modules:
  0.0 119.7 jit_solution(13399093261795162874)
XLA Ops:
  0.6 116.0 %shard_map.149 = (bf16[64,512]{1,0:T(8,128)(2,1)}, f32[3,12,8,32]{3,2,1,0:T(8,128)}) custom-call(bf16[64,4096]{1,0:T(8,128)(2,1)} %hidden.1, bf16[16,8192]{1,0:T(8,128)(2,1)} %bitcast.25, bf16[8,256,512]{2,1,0:T(8,128)(2,1)} %key_cache.1, bf16[8,256,512]{2,1,0:T(8,128)(2,1)} %value_cache.1, bf16[16,512]{1,0:T(8,128)(2,1)} %bitcast.27, ...), custom_call_target="tpu_custom_call" | custom-call | tf_op jit(solution)/shard_map/pallas_call | solution.py:608
  116.7 1.5 %copy.18 = bf16[64,512]{1,0:T(8,128)(2,1)} copy(bf16[64,512]{1,0:T(8,128)(2,1)} %get-tuple-element.8) | data formatting | bytes 131072
  118.2 1.6 %copy.19 = f32[3,8,12,32]{3,1,2,0:T(8,128)} copy(f32[3,8,12,32]{3,1,2,0:T(8,128)} %bitcast.26) | data formatting | bytes 73728

commit v4 on v3

--- a/solution.py
+++ b/solution.py
@@ -22,13 +22,15 @@
 TILES = FF // BLOCK
 COLS = D // BLOCK
 SHARE = D // N_TP
-NEAR = 4 * N_TP
+NEAR = 2 * N_TP
+MATES = 8 * N_TP
 QUARTER = D // 4
 FOLD = 4 * SHARD
 
 neg_fill = -1e30
 epsilon = 1e-06
 fp_limit = 448.0
+EARLY = 1
 tie_nudge = 1.0 + 2.0**-22
 
 f32 = jnp.float32
@@ -71,6 +73,8 @@
     wproj,
     cur,
     mine,
+    other,
+    both,
     x1r,
     every,
     sendw,
@@ -89,10 +93,10 @@
     recve,
     sendg,
     recvg,
-    sendr,
-    recvr,
     spread,
     local_sem,
+    x0s,
+    x0q,
     x1s,
     x1q,
     x2s,
@@ -111,8 +115,6 @@
     eq,
     gs,
     gq,
-    rs,
-    rq,
 ):
     f = lax.axis_index("fsdp")
     t = lax.axis_index("tp")
@@ -120,11 +122,14 @@
     core = lax.rem(f, 2)
     partner = f + 1 - 2 * core
 
+    tp_peers = [lax.rem(t + d, N_TP) for d in range(N_TP)]
+    chip_peers = [lax.rem(k + d, 8) for d in range(8)]
+
     def tp_peer(d):
-        return lax.rem(t + d, N_TP)
+        return tp_peers[d] if isinstance(d, int) else lax.rem(t + d, N_TP)
 
     def chip_peer(d):
-        return lax.rem(k + d, 8)
+        return chip_peers[d] if isinstance(d, int) else lax.rem(k + d, 8)
 
     def remote(src, dst, send, recv, to):
         return pltpu.make_async_remote_copy(
@@ -143,19 +148,25 @@
 
         lax.fori_loop(low, high, step, 0)
 
+    def unrolled(low, high, body):
+        for d in range(low, high):
+            body(d)
+
     barrier = pltpu.get_barrier_semaphore()
 
     def greet(to):
         pl.semaphore_signal(barrier, inc=1, device_id=to, device_id_type=pl.DeviceIdType.MESH)
 
+    def mate(d):
+        return 2 * chip_peer(d // N_TP) + core, tp_peer(d % N_TP)
+
     def near_peer(d):
-        return (f // 4) * 4 + lax.rem(lax.rem(f, 4) + d // N_TP, 4), lax.rem(t + d, N_TP)
-
-    def far_peer(d):
-        return 4 * lax.rem(f // 4 + 1 + d // 2, 4) + 2 * lax.rem(d, 2) + core, t
-
-    each(1, NEAR, lambda d: greet(near_peer(d)))
-    each(0, 6, lambda d: greet(far_peer(d)))
+        side = lax.rem(k, 2)
+        chip = k + (d // N_TP) * (1 - 2 * side)
+        return 2 * chip + core, tp_peer(d % N_TP)
+
+    unrolled(1, MATES, lambda d: greet(mate(d)))
+    greet((partner, t))
 
     own_cols = pl.ds(pl.multiple_of(t * SHARE, SHARE), SHARE)
     loads = [
@@ -233,16 +244,6 @@
     mine[:, :BLOCK] = near_max
     mine[:, BLOCK:] = far_max
 
-    pl.semaphore_wait(barrier, NEAR - 1 + 6)
-
-    place_here = lax.rem(f, 4) * N_TP + t
-
-    def x1(d):
-        return remote(mine, x1r.at[place_here], x1s.at[d], x1q.at[d], near_peer(d))
-
-    each(1, NEAR, lambda d: x1(d).start())
-    x1r[place_here] = mine[...]
-
     for load in loads[:3]:
         load.wait()
     row_of = lax.rem(iota((16, HD), 0), 8)
@@ -287,27 +288,50 @@
             parts = [heads[(half * 8 + h) * 16 : (half * 8 + h + 1) * 16] for h in range(8)]
             sendh[2 * g + half] = jnp.concatenate(parts, axis=1)
 
-    each(0, KVH, attend)
+    each(0, EARLY, attend)
+
+    pl.semaphore_wait(barrier, MATES)
+
+    swap = remote(mine, other, x0s.at[0], x0q.at[0], (partner, t))
+    swap.start()
+    swap.wait_recv()
+    even = lax.rem(k, 2) == 0
+    first = core == 0
+    near_a = jnp.where(first, mine[:, :BLOCK], other[:, :BLOCK])
+    near_b = jnp.where(first, other[:, :BLOCK], mine[:, :BLOCK])
+    far_a = jnp.where(first, mine[:, BLOCK:], other[:, BLOCK:])
+    far_b = jnp.where(first, other[:, BLOCK:], mine[:, BLOCK:])
+    both[:, :BLOCK] = jnp.where(even, jnp.maximum(near_a, near_b), near_a)
+    both[:, BLOCK:] = jnp.where(even, far_b, jnp.maximum(far_a, near_b))
+    place_here = lax.rem(k, 2) * N_TP + t
+
+    def x1(d):
+        return remote(both, x1r.at[place_here], x1s.at[d], x1q.at[d], near_peer(d))
+
+    unrolled(1, NEAR, lambda d: x1(d).start())
+    x1r[place_here] = both[...]
+
+    each(EARLY, KVH, attend)
 
     def send_heads(d):
         return remote(
             sendh.at[tp_peer(d)], recvh.at[t], hs.at[d], hq.at[d], (f, tp_peer(d))
         )
 
-    each(1, N_TP, lambda d: send_heads(d).start())
+    unrolled(1, N_TP, lambda d: send_heads(d).start())
     recvh[t] = sendh[t]
 
     each(1, NEAR, lambda d: x1(d).wait_recv())
     quad = f // 4
-    for tile in range(3):
-        first = x1r[tile * N_TP, :, BLOCK if tile else 0 : 2 * BLOCK if tile else BLOCK]
-        for j in range(N_TP):
-            if tile:
-                first = jnp.maximum(first, x1r[tile * N_TP + j, :, BLOCK:])
-            else:
-                first = jnp.maximum(first, x1r[j, :, :BLOCK])
-            first = jnp.maximum(first, x1r[(tile + 1) * N_TP + j, :, :BLOCK])
-        every[quad, tile] = first
+    maxima = []
+    for side in range(2):
+        whole = x1r[side * N_TP]
+        for j in range(1, N_TP):
+            whole = jnp.maximum(whole, x1r[side * N_TP + j])
+        maxima.append(whole)
+    every[quad, 0] = maxima[0][:, :BLOCK]
+    every[quad, 1] = jnp.maximum(maxima[0][:, BLOCK:], maxima[1][:, :BLOCK])
+    every[quad, 2] = maxima[1][:, BLOCK:]
 
     def x2(d):
         to = 4 * lax.rem(quad + d, 4) + lax.rem(f, 4)
@@ -404,7 +428,6 @@
     pass_on(0).start()
 
     quarter_of = lax.rem(iota((WIN * CAP, 8 * FOLD), 1), FOLD) // SHARD
-    own_share = pl.ds(pl.multiple_of(t * CAP, CAP), CAP)
 
     def send_slots(s, d):
         return remote(
@@ -416,15 +439,18 @@
         return remote(sende.at[s], recve.at[s, k], es.at[s, d], eq.at[s, d], (to, t))
 
     def send_partial(s, d):
-        to = 2 * chip_peer(d) + core
+        to = chip_peer(d // N_TP) * N_TP + tp_peer(d % N_TP)
         return remote(
-            sendg.at[s, chip_peer(d)], recvg.at[s, k], gs.at[s, d], gq.at[s, d], (to, t)
-        )
-
-    def send_back(s, d):
-        return remote(
-            sendr.at[s, tp_peer(d)], recvr.at[s, t], rs.at[s, d], rq.at[s, d], (f, tp_peer(d))
-        )
+            sendg.at[s, pl.ds(pl.multiple_of(to * 16, 16), 16)],
+            recvg.at[s, pl.ds(pl.multiple_of((k * N_TP + t) * 16, 16), 16)],
+            gs.at[s],
+            gq.at[s],
+            mate(d),
+        )
+
+    def all_partials(s):
+        most = slice(0, (MATES - 1) * 16)
+        return remote(sendg.at[s, most], recvg.at[s, most], gs.at[s], gq.at[s], (partner, t))
 
     def gathered(s, half, m):
         rows = recve[s].reshape(128, 2048)
@@ -445,6 +471,12 @@
         split = split.reshape(3, WIN * CAP, 8 * FOLD)
         return split[0] + split[1] + split[2]
 
+    def drain_early(d):
+        send_heads(d).wait_send()
+        for m in range(3):
+            send_weights(m, d).wait_send()
+        send_projected(0, d).wait_send()
+
     def decode(s):
         each(1, N_TP, lambda d: send_projected(s, d).wait_recv())
         projected = recvp[s, 0].astype(f32)
@@ -453,7 +485,7 @@
         mix = (cur[...].astype(f32) + projected).astype(bf16)
         mixed[s] = mix
         sendd[s] = nn_dot(slots[s], mix).reshape(WIN, CAP, SHARE)
-        each(1, N_TP, lambda d: send_slots(s, d).start())
+        unrolled(1, N_TP, lambda d: send_slots(s, d).start())
         recvd[s, t] = sendd[s, t]
         each(1, N_TP, lambda d: send_slots(s, d).wait_recv())
         blocks = [recvd[s, j] for j in range(N_TP)]
@@ -469,11 +501,17 @@
             [jnp.concatenate(normed[:4], axis=1), jnp.concatenate(normed[4:], axis=1)], axis=0
         ).astype(bf16)
         sende[s] = folded
-        each(1, 8, lambda d: send_normed(s, d).start())
+        unrolled(1, 8, lambda d: send_normed(s, d).start())
         recve[s, k] = folded
 
         @pl.when(s == 0)
         def _():
+            each(1, 4, lambda d: x2(d).wait_recv())
+            for tile in range(TILES):
+                log = jnp.log2((every[tile // 3, tile % 3] + epsilon) / fp_limit)
+                for m in range(3):
+                    logs[m, tile] = log[:, m * COLS : (m + 1) * COLS]
+
             def forward(d):
                 for m in range(3):
                     send_weights(m, d).wait_recv()
@@ -494,48 +532,47 @@
             ).astype(bf16)
             total = total + nn_dot(stacked, wbuf[half, 2].reshape(8 * FOLD, QUARTER))
         total = total.reshape(4, 8, CAP, QUARTER)
-        halves = [jnp.concatenate([total[2 * h], total[2 * h + 1]], axis=2) for h in range(2)]
-        sendg[s] = jnp.concatenate(halves, axis=1).astype(bf16)
-        each(1, 8, lambda d: send_partial(s, d).start())
-        recvg[s, k] = sendg[s, k]
-        each(1, 8, lambda d: send_partial(s, d).wait_recv())
-        summed = recvg[s, 0].astype(f32)
+        folds = []
+        for j in range(N_TP):
+            block = total[j // 2, :, :, (j % 2) * SHARE : (j % 2 + 1) * SHARE]
+            folds.append(jnp.concatenate([block[..., : SHARE // 2], block[..., SHARE // 2 :]], axis=1))
+        folds = jnp.stack(folds, axis=1).astype(bf16)
+        sendg[s] = folds.reshape(MATES * 16, SHARE // 2)
+        unrolled(1, MATES, lambda d: send_partial(s, d).start())
+        here = pl.ds(pl.multiple_of((k * N_TP + t) * 16, 16), 16)
+        recvg[s, here] = sendg[s, here]
+
+        @pl.when(s == 0)
+        def _():
+            swap.wait_send()
+            each(1, NEAR, lambda d: x1(d).wait_send())
+            each(1, 4, lambda d: x2(d).wait_send())
+            each(0, N_TP, lambda d: pass_on(d).wait_send())
+            each(1, N_TP, drain_early)
+
+        all_partials(s).wait_recv()
+        block_rows = N_TP * 16
+        summed = recvg[s, :block_rows].astype(f32)
         for j in range(1, 8):
-            summed = summed + recvg[s, j].astype(f32)
-        summed = summed.reshape(2, CAP, 2048) * share[s, own_share, :1][None]
-        for j in range(N_TP):
-            sendr[s, j] = summed[j // 4, :, (j % 4) * SHARE : (j % 4 + 1) * SHARE]
-        each(1, N_TP, lambda d: send_back(s, d).start())
-        recvr[s, t] = sendr[s, t]
-        each(1, N_TP, lambda d: send_back(s, d).wait_recv())
-        returned = recvr[s].reshape(WIN * CAP, SHARE).astype(bf16)
+            summed = summed + recvg[s, j * block_rows : (j + 1) * block_rows].astype(f32)
+        summed = summed.reshape(WIN, 2, CAP, SHARE // 2)
+        summed = jnp.concatenate([summed[:, 0], summed[:, 1]], axis=2).reshape(WIN * CAP, SHARE)
+        returned = (summed * share[s, :, :1]).astype(bf16)
         moe = nn_dot(slots_t[s], returned)
         cur[...] = (mixed[s].astype(f32) + moe).astype(bf16)
 
     each(0, STEPS, decode)
     out[...] = cur[...]
 
-    each(1, 4, lambda d: x2(d).wait_recv())
-    for tile in range(TILES):
-        log = jnp.log2((every[tile // 3, tile % 3] + epsilon) / fp_limit)
-        for m in range(3):
-            logs[m, tile] = log[:, m * COLS : (m + 1) * COLS]
-    each(1, 4, lambda d: x2(d).wait_send())
-    each(1, NEAR, lambda d: x1(d).wait_send())
-    each(0, N_TP, lambda d: pass_on(d).wait_send())
-
     def drain(d):
-        send_heads(d).wait_send()
-        for m in range(3):
-            send_weights(m, d).wait_send()
+        send_projected(1, d).wait_send()
         for s in range(STEPS):
-            send_projected(s, d).wait_send()
             send_slots(s, d).wait_send()
             send_normed(s, d).wait_send()
-            send_partial(s, d).wait_send()
-            send_back(s, d).wait_send()
 
     each(1, N_TP, drain)
+    for s in range(STEPS):
+        all_partials(s).wait_send()
 
 
 def local(
@@ -571,6 +608,8 @@
         v((QH * HD // N_TP, D), bf16),
         v((ROWS, SHARE), bf16),
         v((WIN, 2 * BLOCK), f32),
+        v((WIN, 2 * BLOCK), f32),
+        v((WIN, 2 * BLOCK), f32),
         v((NEAR, WIN, 2 * BLOCK), f32),
         v((4, 3, WIN, BLOCK), f32),
         v((3, N_TP, FOLD, QUARTER), bf16),
@@ -587,12 +626,12 @@
         v((STEPS, N_TP, CAP, SHARE), f32),
         v((STEPS, 16, 2048), bf16),
         v((STEPS, 8, 16, 2048), bf16),
-        v((STEPS, 8, 16, 2048), bf16),
-        v((STEPS, 8, 16, 2048), bf16),
-        v((STEPS, N_TP, CAP, SHARE), f32),
-        v((STEPS, N_TP, CAP, SHARE), f32),
+        v((STEPS, MATES * 16, SHARE // 2), bf16),
+        v((STEPS, MATES * 16, SHARE // 2), bf16),
         v((8 * FOLD, 8 * FOLD), bf16),
         dma((8,)),
+        dma((1,)),
+        dma((1,)),
         dma((NEAR,)),
         dma((NEAR,)),
         dma((4,)),
@@ -604,7 +643,8 @@
         dma((N_TP,)),
         dma((N_TP,)),
     ]
-    scratch += [dma((STEPS, N_TP)) for _ in range(10)]
+    scratch += [dma((STEPS, N_TP)) for _ in range(6)]
+    scratch += [dma((STEPS,)) for _ in range(2)]
     out, logs = pl.pallas_call(
         kernel,
         out_shape=(

time: 120 us -> 113 us (0.942)
  Pallas kernels: 116 us -> 109 us
    pallas_call x1, Pallas kernels: 116 us -> 109 us  [local(): pl.pallas_call(kernel, out_shape=(jax.ShapeDtypeStruct((ROWS, SHARE), bf1...]
where the time goes in v4:
time: 113 us
  Pallas kernels  109 us (96%)
  local copies, waits for them, and re-layouts  3.05 us (3%)
    pallas_call x1, Pallas kernels, local(): pl.pallas_call(kernel, out_shape=(jax.ShapeDtypeStruct((ROWS, SHARE), bf1...  109 us
    unnamed x2, local copies, waits for them, and re-layouts  3.05 us

profile of v4, /device:TPU:0, one launch (start us, length us, event | category | flops | bytes accessed | tf_op | source)
XLA Modules:
  0.0 112.8 jit_solution(18437332300541269677)
XLA Ops:
  0.6 109.1 %shard_map.149 = (bf16[64,512]{1,0:T(8,128)(2,1)}, f32[3,12,8,32]{3,2,1,0:T(8,128)}) custom-call(bf16[64,4096]{1,0:T(8,128)(2,1)} %hidden.1, bf16[16,8192]{1,0:T(8,128)(2,1)} %bitcast.25, bf16[8,256,512]{2,1,0:T(8,128)(2,1)} %key_cache.1, bf16[8,256,512]{2,1,0:T(8,128)(2,1)} %value_cache.1, bf16[16,512]{1,0:T(8,128)(2,1)} %bitcast.27, ...), custom_call_target="tpu_custom_call" | custom-call | tf_op jit(solution)/shard_map/pallas_call | solution.py:648
  109.7 1.5 %copy.18 = bf16[64,512]{1,0:T(8,128)(2,1)} copy(bf16[64,512]{1,0:T(8,128)(2,1)} %get-tuple-element.8) | data formatting | bytes 131072
  111.2 1.6 %copy.19 = f32[3,8,12,32]{3,1,2,0:T(8,128)} copy(f32[3,8,12,32]{3,1,2,0:T(8,128)} %bitcast.26) | data formatting | bytes 73728
